TPU v7x, 512 devices: a whole 4x4x16 slice. The times are simulated.
512 devices in a mesh: src: 64 (over z, x), tm: 8 (over y, core).
Axes of the slice: x: 4, y: 4, z: 16, core: 2. Of those that a mesh axis runs over, the one named last changes fastest.
Arguments:
- waveforms: bfloat16 [16, 2048, 8192], P('tm', 'src'), may hold values from -6 to 6
- scen_weights: bfloat16 [1024, 2048], P(None, 'src'), may hold values from -0.125 to 0.125
- rates: float32 [1024], replicated, may hold values from 0.1 to 4
- tile_cells: int32 [8192], replicated, may hold values from 0 to 8191, each once
- level_base: int32 [8192], P('src'), may hold values from 0 to 7
- wet_mask: int32 [8192], P('src'), may hold values 0 or 1
Outputs:
- hazard: float32 [16, 8192], P('tm', 'src')
Inputs may be any that keep to these rules, and one draw needn't show every extreme that they name: `tile_cells`: each cell appears exactly once.
All inputs are finite; a program needn't handle non-finite values. No bound on the sum of `wet_mask` on one device may be relied on, other than what follows from the above.
Results may differ from a plain program's by a relative error of at most 0.0003.
Values may be sent and summed in bfloat16 or wider, within the bound.
No kernel may reach another device: no remote copies, remote signals or barrier semaphores. Data moves between devices by JAX's collectives and lax.ppermute only.
A program may use at most 64 MiB of HBM per device.

v0:
```python
import jax
import jax.numpy as jnp
from jax import lax
from jax.sharding import PartitionSpec as P

K = 1024
NB = 16


def exceedance(peak, rate_part, level_base, first_level, count):
    log_amp = jnp.log(jnp.maximum(peak, 0.1))
    base = level_base.astype(jnp.float32)
    scale = 1.0 / (0.5 * jnp.sqrt(jnp.float32(2.0)))

    def one_level(level):
        log_level = jnp.log(jnp.float32(0.1)) + 0.15 * (
            base + (first_level + level).astype(jnp.float32)
        )
        exceed = 0.5 * jax.scipy.special.erfc((log_level[None, :] - log_amp) * scale)
        return jnp.dot(rate_part, exceed, precision=lax.Precision.HIGHEST) / K

    return lax.map(one_level, jnp.arange(count, dtype=jnp.int32))


def body(waveforms, scen_weights, rates, tile_cells, level_base, wet_mask):
    tiled = jnp.take(waveforms, tile_cells, axis=2)
    weights_all = lax.all_gather(scen_weights, "src", axis=1, tiled=True)
    eta = jnp.einsum(
        "ks,tsc->tkc",
        weights_all,
        lax.all_to_all(tiled, "src", split_axis=2, concat_axis=1, tiled=True),
        preferred_element_type=jnp.float32,
    )
    peak_local = jnp.max(eta, axis=0)
    levels_dev = NB // lax.axis_size("tm")
    peak = lax.pmax(peak_local, "tm")
    first_level = lax.axis_index("tm") * levels_dev
    hazard = exceedance(peak, rates, level_base, first_level, levels_dev)
    return hazard * wet_mask.astype(jnp.float32)[None, :]


def solution(mesh):
    return jax.shard_map(
        body,
        mesh=mesh,
        in_specs=(P("tm", "src", None), P(None, "src"), P(), P(), P("src"), P("src")),
        out_specs=P("tm", "src"),
        check_vma=False,
    )
```

profile of v0, /device:TPU:1, one launch (start us, length us, event | category | flops | bytes accessed | tf_op | source)
XLA Modules:
  0.0 292.1 jit_solution(11703241638383345429)
XLA Ops:
  6.5 0.0 copy-start
  6.5 0.0 all-gather.2.cloned.1.call-start
  6.5 0.7 all-gather.2.cloned.1.call-update
  7.3 0.0 all-reduce.2.cloned.1.call-start
  7.3 9.2 %copy.11 = bf16[2,32,8192]{1,0,2:T(2,128)(2,1)} copy(bf16[2,32,8192]{2,1,0:T(8,128)(2,1)} %param.8) | data formatting | bytes 2097152 | tf_op args[0]
  16.5 0.0 copy-done
  16.5 55.5 %gather_fusion = bf16[8192,2,32]{2,1,0:T(2,128)(2,1)} fusion(bf16[2,32,8192]{1,0,2:T(2,128)(2,1)} %copy.11, s32[8192]{0:T(1024)S(1)} %fusion.125), kind=kCustom, calls=%fused_computation | custom fusion | bytes 2129920 | tf_op jit(solution)/shard_map/jit(_take)/gather | solution.py:26
  72.0 30.8 %fusion.126 = bf16[8192,2,32]{2,1,0:T(2,128)(2,1)} fusion(bf16[8192,2,32]{2,1,0:T(2,128)(2,1)} %gather_fusion, pred[8192]{0:T(1024)(128)(4,1)S(1)} %compare_and_fusion), kind=kLoop, calls=%fused_computation.138 | loop fusion | flops 524288 | bytes 2105344
  102.9 9.1 %reshape.23 = bf16[64,2,4096]{2,1,0:T(2,128)(2,1)S(1)} reshape(bf16[8192,2,32]{2,1,0:T(2,128)(2,1)} %fusion.126) | data formatting | bytes 2097152
  112.0 79.9 %all_to_all.18 = bf16[64,2,4096]{2,1,0:T(2,128)(2,1)S(1)} all-to-all(bf16[64,2,4096]{2,1,0:T(2,128)(2,1)S(1)} %reshape.23), channel_id=1, replica_groups=mesh['src'=64,'tm'=8] {'src'}, dimensions={0} | all-to-all | bytes 2097152 | tf_op jit(solution)/shard_map/all_to_all | solution.py:31
  192.0 3.5 %reshape.24 = bf16[8192,2,32]{2,1,0:T(2,128)(2,1)} reshape(bf16[64,2,4096]{2,1,0:T(2,128)(2,1)S(1)} %all_to_all.18) | data formatting | bytes 2097152
  195.5 8.4 %copy.12 = bf16[2,32,64,128]{3,1,2,0:T(8,128)(2,1)S(1)} copy(bf16[2,32,64,128]{1,0,3,2:T(2,128)(2,1)} %bitcast.39) | data formatting | bytes 2097152 | tf_op jit(solution)/shard_map/all_to_all | solution.py:31
  203.9 0.0 copy-start.2
  203.9 0.0 copy-start.3
  203.9 0.0 all-gather.2.cloned.1.call-done
  204.0 0.0 copy-start.1
  204.0 4.3 %fusion.122 = f32[128,1024]{1,0:T(8,128)} fusion(bf16[2,2048,128]{2,1,0:T(8,128)(2,1)S(1)} %bitcast.40, bf16[1024,2048]{0,1:T(8,128)(2,1)} %all-gather.2.cloned.1.call-done), kind=kOutput, calls=%fused_computation.132 | convolution fusion | flops 1073872896 | bytes 5767168 | tf_op jit(solution)/shard_map/ks,tsc->tkc/dot_general | solution.py:28
  208.3 0.0 all-reduce.2.cloned.1.call-update
  208.3 0.0 copy-done.2
  208.3 0.0 copy-done.3
  208.4 69.6 %all-reduce.2.cloned.1.call-done = f32[1024,128]{0,1:T(8,128)} async-done(((f32[1024,128]{0,1:T(8,128)}), f32[1024,128]{0,1:T(8,128)}) %all-reduce.2.cloned.1.call-update) | async-done | bytes 524304 | tf_op jit(solution)/shard_map/pmax | solution.py:36
  278.0 1.1 maximum_log_fusion
  279.1 0.2 copy.14
  279.3 0.0 copy-done.1
  279.3 5.4 %while.10 = (s32[]{:T(128)}, f32[2,128]{1,0:T(2,128)S(1)}, s32[2]{0:T(128)S(1)}, s32[]{:T(128)}, f32[128]{0:T(128)S(1)}, /*index=5*/f32[1024,128]{1,0:T(8,128)S(1)}, f32[1024]{0:T(1024)S(1)}, s32[]{:T(128)}, s32[]{:T(128)}) while((s32[]{:T(128)}, f32[2,128]{1,0:T(2,128)S(1)}, s32[2]{0:T(128)S(1)}, s32[]{:T(128)}, f32[128]{0:T(128)S(1)}, ...), condition=%wide.region_3.4_spmd, body=%wide.region_2.3_spmd.sunk | while | flops 9830916 | bytes 531589 | solution.py:22
  279.3 0.6 dynamic_slice.5
  280.5 1.5 fusion.134
  282.0 0.6 dynamic_slice.5
  283.2 1.5 fusion.134
  284.7 0.6 broadcast_multiply_fusion
  (10 shorter events, 0.1 us)
Async XLA Ops:
  6.5 10.0 %copy-start = (s32[8192]{0:T(1024)S(1)}, s32[8192]{0:T(1024)}, u32[]{:S(2)}) copy-start(s32[8192]{0:T(1024)} %param.11) | copy-start | bytes 98308
  6.5 197.4 %all-gather.2.cloned.1.call-start = ((), (), s32[]{:S(2)}) async-start(), calls=%async_computation.1 | async-start | bytes 4259840 | tf_op jit(solution)/shard_map/all_gather | solution.py:27
  7.3 270.7 %all-reduce.2.cloned.1.call-start = ((), (), s32[]{:S(2)}) async-start(), calls=%async_computation.2 | async-start | bytes 1048576 | tf_op jit(solution)/shard_map/pmax | solution.py:36
  203.9 4.4 %copy-start.2 = (s32[128]{0:T(128)S(1)}, s32[128]{0:T(128)}, u32[]{:S(2)}) copy-start(s32[128]{0:T(128)} %param.12) | copy-start | bytes 1540
  203.9 4.4 %copy-start.3 = (s32[128]{0:T(128)S(1)}, s32[128]{0:T(128)}, u32[]{:S(2)}) copy-start(s32[128]{0:T(128)} %param.13) | copy-start | bytes 1540
  204.0 75.4 %copy-start.1 = (f32[1024]{0:T(1024)S(1)}, f32[1024]{0:T(1024)}, u32[]{:S(2)}) copy-start(f32[1024]{0:T(1024)} %param.10) | copy-start | bytes 12292
Sparse Core Ops, SparseCore 0:
  10.3 175.0 all-gather.1
  208.4 69.5 all-reduce.1
where the time goes:
time: 294 us; the launch traced here: 292 us
  local copies, waits for them, and re-layouts  87.2 us (30%)
  blocking collectives  79.9 us (27%)
  waiting for transfers between devices  70.4 us (24%)
  other arithmetic  32.6 us (11%)
  between operations  13.5 us (5%)
  matrix products  7.3 us (2%)
    all_to_all x1, blocking collectives, body(): lax.all_to_all(tiled, 'src', split_axis=2, concat_axis=1, tiled=True)  79.9 us
    pmax x1, waiting for transfers between devices, body(): peak = lax.pmax(peak_local, 'tm')  69.6 us
    gather x1, local copies, waits for them, and re-layouts, body(): tiled = jnp.take(waveforms, tile_cells, axis=2)  55.5 us
    unnamed x1, other arithmetic  30.8 us
    unnamed x11, local copies, waits for them, and re-layouts  21.9 us
    all_to_all x1, local copies, waits for them, and re-layouts, body(): lax.all_to_all(tiled, 'src', split_axis=2, concat_axis=1, tiled=True)  8.37 us
  transfers between devices with their start and end apart: 2, of which 1 were waited for; matrix products, arithmetic and copies ran while one was open for 40% of the time, Pallas kernels for 0%

commit v1 on v0

v1 whole, which is shorter than its diff:
```python
import functools

import jax
import jax.numpy as jnp
from jax import lax
from jax.experimental import pallas as pl
from jax.experimental.pallas import tpu as pltpu
from jax.sharding import Mesh, PartitionSpec as P

K = 1024
NB = 16
C = 8192
EVERY = ("z", "x", "y", "c")
MIB = 1 << 20

ERFC_P = (
    2.326819970068386e-2,
    -1.387039388740657e-1,
    3.687424674597105e-1,
    -5.824733027278666e-1,
    6.210004621745983e-1,
    -4.944515323274145e-1,
    3.404879937665872e-1,
    -2.741127028184656e-1,
    5.638259427386472e-1,
)
ERFC_R = (
    -1.047766399936249e1,
    1.297719955372516e1,
    -7.495518717768503e0,
    2.921019019210786e0,
    -1.015265279202700e0,
    4.218463358204948e-1,
    -2.820767439740514e-1,
    5.641895067754075e-1,
)
ERF_T = (
    7.853861353153693e-5,
    -8.010193625184903e-4,
    5.188327685732524e-3,
    -2.685381193529856e-2,
    1.128358514861418e-1,
    -3.761262582423300e-1,
    1.128379165726710e0,
)


def poly(x, coefficients):
    total = jnp.full_like(x, coefficients[0])
    for c in coefficients[1:]:
        total = total * x + c
    return total


def erfc(x):
    square = x * x
    inner = 1.0 - x * poly(square, ERF_T)
    size = jnp.maximum(jnp.abs(x), 1.0)
    inverse = 1.0 / size
    q = inverse * inverse
    tail = jnp.exp(-square) * inverse * jnp.where(size < 2.0, poly(q, ERFC_P), poly(q, ERFC_R))
    outer = jnp.where(x < 0.0, 2.0 - tail, tail)
    return jnp.where(jnp.abs(x) < 1.0, inner, outer)


def gather_kernel(cells_ref, wave_ref, out_ref, turned, picked):
    half = C // 2

    @pl.loop(0, half // 128)
    def _(j):
        low = wave_ref[:, pl.ds(pl.multiple_of(j * 128, 128), 128)]
        high = wave_ref[:, pl.ds(pl.multiple_of(half + j * 128, 128), 128)]
        both = jnp.concatenate([low.astype(jnp.float32), high.astype(jnp.float32)], axis=0).T
        turned[pl.ds(pl.multiple_of(j * 128, 128), 128), :] = both
        turned[pl.ds(pl.multiple_of(half + j * 128, 128), 128), :] = pltpu.roll(both, 64, 1)

    first = lax.broadcasted_iota(jnp.int32, (1, 128), 1) < 64

    @pl.loop(0, C // 32)
    def _(pair):
        for e in range(2):
            for a in range(8):
                at = pair * 32 + e * 16 + a
                one = turned[pl.ds(cells_ref[at], 1), :]
                two = turned[pl.ds(cells_ref[at + 8] ^ half, 1), :]
                picked[pl.ds(pair * 16 + e * 8 + a, 1), :] = jnp.where(first, one, two)

    @pl.loop(0, C // 2 // 128)
    def _(i):
        rows = pl.ds(pl.multiple_of(i * 128, 128), 128)
        out_ref[rows, :] = picked[rows, :].astype(jnp.bfloat16)


def gather(cells, wave):
    return pl.pallas_call(
        gather_kernel,
        out_shape=jax.ShapeDtypeStruct((C // 2, 128), jnp.bfloat16),
        in_specs=[pl.BlockSpec(memory_space=pltpu.SMEM), pl.BlockSpec(memory_space=pltpu.VMEM)],
        out_specs=pl.BlockSpec(memory_space=pltpu.VMEM),
        scratch_shapes=[pltpu.VMEM((C, 128), jnp.float32), pltpu.VMEM((C // 2, 128), jnp.float32)],
        compiler_params=pltpu.CompilerParams(vmem_limit_bytes=32 * MIB),
        cost_estimate=pl.CostEstimate(flops=1 << 20, bytes_accessed=40 * MIB, transcendentals=0),
        name="gather_cells",
    )(cells, wave)


def hazard_kernel(got_ref, weights_ref, rates_ref, base_ref, out_ref, columns, weights, logs, sem):
    copy = pltpu.make_async_copy(weights_ref, weights, sem)
    copy.start()
    lane = lax.broadcasted_iota(jnp.int32, (16, 128), 1)
    in64 = lane < 64
    in32 = (lane & 63) < 32

    def swap(one, two, shift, mask):
        return (
            jnp.where(mask, one, pltpu.roll(two, shift, 1)),
            jnp.where(mask, pltpu.roll(one, 128 - shift, 1), two),
        )

    @pl.loop(0, 4)
    def _(x):
        for y in range(4):
            for zq in range(4):
                tiles = []
                for i in range(4):
                    row = (4 * zq + i) * 256 + x * 64 + y * 16
                    tiles.append(got_ref[pl.ds(pl.multiple_of(row, 16), 16), :].astype(jnp.float32))
                v0, v2 = swap(tiles[0], tiles[2], 64, in64)
                v1, v3 = swap(tiles[1], tiles[3], 64, in64)
                w0, w1 = swap(v0, v1, 32, in32)
                w2, w3 = swap(v2, v3, 32, in32)
                for c in range(2):
                    part = slice(8 * c, 8 * c + 8)
                    for t, (early, late) in enumerate(((w0, w2), (w1, w3))):
                        block = jnp.concatenate([early[part], late[part]], axis=0)
                        at = ((2 * y + c) * 2 + t) * 16
                        columns[at : at + 16, pl.ds(pl.multiple_of(x * 512 + zq * 128, 128), 128)] = block.astype(jnp.bfloat16)

    copy.wait()
    for n in range(4):
        total = jnp.zeros((256, 256), jnp.float32)
        for x in range(4):
            at = (x * 8 + 2 * n) * 512
            right = jnp.concatenate([weights[at : at + 512, :], weights[at + 512 : at + 1024, :]], axis=1)
            total += jnp.dot(columns[:, x * 512 : (x + 1) * 512], right, preferred_element_type=jnp.float32)
        peak = total[0:16]
        for t in range(1, 16):
            peak = jnp.maximum(peak, total[t * 16 : (t + 1) * 16])
        logs[:, n * 256 : (n + 1) * 256] = jnp.log(jnp.maximum(peak, 0.1))

    log_amp = logs[...]
    scale = 1.0 / (0.5 * jnp.sqrt(jnp.float32(2.0)))
    bottom = jnp.log(jnp.full((16, 128), 0.1, jnp.float32))
    rates = rates_ref[...]
    base = base_ref[...]

    def level(j, result):
        log_level = (bottom + 0.15 * (base + j.astype(jnp.float32)))[:, 0:1]
        value = rates * erfc((log_level - log_amp) * scale)
        hazard = jnp.sum(value, axis=1, keepdims=True) * (0.5 / K)
        return jnp.where(lane == j, hazard, result)

    out_ref[...] = lax.fori_loop(0, NB, level, jnp.zeros((16, 128), jnp.float32))


def hazard_of(got, weights, rates, base):
    vmem = pl.BlockSpec(memory_space=pltpu.VMEM)
    return pl.pallas_call(
        hazard_kernel,
        out_shape=jax.ShapeDtypeStruct((16, 128), jnp.float32),
        in_specs=[vmem, pl.BlockSpec(memory_space=pl.ANY), vmem, vmem],
        out_specs=vmem,
        scratch_shapes=[
            pltpu.VMEM((256, 2048), jnp.bfloat16),
            pltpu.VMEM((16384, 128), jnp.bfloat16),
            pltpu.VMEM((16, 1024), jnp.float32),
            pltpu.SemaphoreType.DMA,
        ],
        compiler_params=pltpu.CompilerParams(vmem_limit_bytes=32 * MIB),
        name="hazard_levels",
    )(got, weights, rates, base)


def body(waveforms, scen_weights, rates, tile_cells, level_base, wet_mask):
    me = lax.axis_index(("y", "c"))
    eighth = lax.dynamic_slice_in_dim(scen_weights.T, me * 128, 128, axis=1)
    shared = lax.all_to_all(jnp.broadcast_to(eighth[None], (16, 32, 128)), "z", 0, 0, tiled=True)
    sent = gather(tile_cells, waveforms.reshape(64, C))
    weights = lax.all_gather(shared.reshape(512, 128), ("x", "y", "c"), axis=0, tiled=True)
    got = lax.all_to_all(sent.reshape(512, 8, 128), EVERY, 0, 0, tiled=True)
    base = lax.dynamic_slice_in_dim(level_base.astype(jnp.float32), me * 16, 16)
    base = jnp.broadcast_to(base[:, None], (16, 128))
    part = hazard_of(got.reshape(C // 2, 128), weights, rates.reshape(1, K), base)
    levels = part[:, :NB].reshape(16, 8, 2).transpose(1, 2, 0)
    hazard = lax.all_to_all(levels, ("y", "c"), 0, 0, tiled=True).transpose(1, 0, 2).reshape(2, 128)
    return hazard * wet_mask.astype(jnp.float32)[None, :]


def solution(mesh):
    split = Mesh(mesh.devices.reshape(16, 4, 4, 2), EVERY)
    src, tm = ("z", "x"), ("y", "c")
    return jax.shard_map(
        body,
        mesh=split,
        in_specs=(P(tm, src, None), P(None, src), P(), P(), P(src), P(src)),
        out_specs=P(tm, src),
        check_vma=False,
    )
```

time: 294 us -> 154 us (0.52)
  local copies, waits for them, and re-layouts: 87.2 us -> 5.93 us
  blocking collectives: 79.9 us -> 27.6 us
  other arithmetic: 32.6 us -> 0.58 us
  Pallas kernels: 0 us -> 24.9 us
  starting transfers between devices: 0.04 us -> 18.4 us
  waiting for transfers between devices: 70.4 us -> 62.4 us
  matrix products: 7.3 us -> 0 us
    pmax x1 -> x0, waiting for transfers between devices: 69.6 us -> none  [body(): peak = lax.pmax(peak_local, 'tm')]
    all_to_all x0 -> x2, waiting for transfers between devices: none -> 62.4 us  [the longest x1 58 us: body(): got = lax.all_to_all(sent.reshape(512, 8, 128), EVERY, 0, 0, tiled=True)]
    gather x1 -> x0, local copies, waits for them, and re-layouts: 55.5 us -> none  [body(): tiled = jnp.take(waveforms, tile_cells, axis=2)]
    all_to_all x1, blocking collectives: 79.9 us -> 27.6 us  [body(): lax.all_to_all(jnp.broadcast_to(eighth[None], (16, 32, 128)), 'z', 0, 0,...]
    unnamed x1 -> x0, other arithmetic: 30.8 us -> none
    pallas_call x0 -> x2, Pallas kernels: none -> 24.9 us  [the longest x1 16.5 us: gather(): pl.pallas_call(gather_kernel, out_shape=jax.ShapeDtypeStruct((C // 2, 128...]
    all_to_all x0 -> x2, starting transfers between devices: none -> 18.4 us  [the longest x1 15.1 us: body(): got = lax.all_to_all(sent.reshape(512, 8, 128), EVERY, 0, 0, tiled=True)]
    unnamed x11 -> x14, local copies, waits for them, and re-layouts: 21.9 us -> 5 us
  transfers between devices with their start and end apart: 2 -> 3, of which waited for: 1 -> 2; matrix products, arithmetic and copies ran while one was open for 40% -> 0% of each run, Pallas kernels for 0% -> 11%
where the time goes in v1:
time: 154 us; the launch traced here: 153 us
  waiting for transfers between devices  62.4 us (41%)
  blocking collectives  27.6 us (18%)
  Pallas kernels  24.9 us (16%)
  starting transfers between devices  18.4 us (12%)
  between operations  13.5 us (9%)
  local copies, waits for them, and re-layouts  5.93 us (4%)
    all_to_all x1, waiting for transfers between devices, body(): got = lax.all_to_all(sent.reshape(512, 8, 128), EVERY, 0, 0, tiled=True)  58 us
    all_to_all x1, blocking collectives, body(): lax.all_to_all(jnp.broadcast_to(eighth[None], (16, 32, 128)), 'z', 0, 0,...  27.6 us
    pallas_call x1, Pallas kernels, gather(): pl.pallas_call(gather_kernel, out_shape=jax.ShapeDtypeStruct((C // 2, 128...  16.5 us
    all_to_all x1, starting transfers between devices, body(): got = lax.all_to_all(sent.reshape(512, 8, 128), EVERY, 0, 0, tiled=True)  15.1 us
    pallas_call x1, Pallas kernels, hazard_of(): pl.pallas_call(hazard_kernel, out_shape=jax.ShapeDtypeStruct((16, 128), j...  8.4 us
    unnamed x14, local copies, waits for them, and re-layouts  5 us
    all_to_all x1, waiting for transfers between devices, body(): lax.all_to_all(levels, ('y', 'c'), 0, 0, tiled=True).transpose(1, 0, 2)  4.35 us
    all_to_all x1, starting transfers between devices, body(): lax.all_to_all(levels, ('y', 'c'), 0, 0, tiled=True).transpose(1, 0, 2)  3.26 us
  transfers between devices with their start and end apart: 3, of which 2 were waited for; matrix products, arithmetic and copies ran while one was open for 0% of the time, Pallas kernels for 11%

profile of v1, /device:TPU:1, one launch (start us, length us, event | category | flops | bytes accessed | tf_op | source)
XLA Modules:
  0.0 153.3 jit_solution(164223014095527096)
XLA Ops:
  6.5 0.0 copy-start
  6.5 0.0 copy-start.5
  6.5 0.0 copy-start.4
  6.5 0.0 all-gather.2.cloned.1.call-start
  6.6 0.8 copy-done
  7.4 27.6 %all_to_all.15 = bf16[16,32,128]{2,1,0:T(8,128)(2,1)} all-to-all(bf16[16,32,128]{2,1,0:T(8,128)(2,1)S(1)} %broadcast_in_dim.4), channel_id=1, replica_groups=mesh['z'=16,'x'=4,'y'=4,'c'=2] {'z'}, dimensions={0} | all-to-all | bytes 262144 | tf_op jit(solution)/shard_map/all_to_all | solution.py:187
  35.1 0.0 all-gather.2.cloned.1.call-update
  35.1 0.0 copy-start.2
  35.1 1.2 copy-done.2
  36.3 0.0 copy-start.3
  36.3 0.8 copy-done.3
  37.1 16.5 %gather_cells.1 = bf16[4096,128]{1,0:T(8,128)(2,1)} custom-call(s32[8192]{0:T(1024)S(1)} %copy-done.3, bf16[64,8192]{1,0:T(8,128)(2,1)S(1)} %bitcast.13), custom_call_target="tpu_custom_call" | custom-call | flops 1048576 | bytes 41943040 | tf_op jit(solution)/shard_map/gather_cells/pallas_call | solution.py:95
  53.6 0.0 copy-start.6
  53.6 15.1 %all-to-all-start = ((bf16[512,8,128]{2,1,0:T(8,128)(2,1)}), bf16[512,8,128]{2,1,0:T(8,128)(2,1)S(1)}, u32[]{:S(2)}, u32[]{:S(2)}) async-start(bf16[512,8,128]{2,1,0:T(8,128)(2,1)} %bitcast.1), calls=%async_computation | async-start | bytes 2097152 | tf_op jit(solution)/shard_map/all_to_all | solution.py:190
  68.7 0.0 copy-done.5
  68.7 0.1 dynamic_slice.7
  68.8 58.0 %all-to-all-done = bf16[512,8,128]{2,1,0:T(8,128)(2,1)S(1)} async-done(((bf16[512,8,128]{2,1,0:T(8,128)(2,1)}), bf16[512,8,128]{2,1,0:T(8,128)(2,1)S(1)}, u32[]{:S(2)}, u32[]{:S(2)}) %all-to-all-start) | async-done | bytes 1048608 | tf_op jit(solution)/shard_map/all_to_all | solution.py:190
  126.8 0.0 all-gather.2.cloned.1.call-done.weights_ref
  126.8 0.1 broadcast_in_dim.5.base_ref
  126.9 0.0 copy-done.4
  126.9 0.0 copy-start.1
  126.9 2.2 %copy-done.1 = bf16[16384,128]{1,0:T(8,128)(2,1)S(1)} copy-done((bf16[16384,128]{1,0:T(8,128)(2,1)S(1)}, bf16[16384,128]{1,0:T(8,128)(2,1)}, u32[]{:S(2)}) %copy-start.1) | copy-done | bytes 4194328
  129.1 8.4 %hazard_levels.1 = f32[16,128]{1,0:T(8,128)S(1)} custom-call(bf16[4096,128]{1,0:T(8,128)(2,1)S(1)} %bitcast.12, bf16[16384,128]{1,0:T(8,128)(2,1)S(1)} %copy-done.1, f32[1,1024]{1,0:T(1,128)S(1)} %bitcast.15, f32[16,128]{1,0:T(8,128)S(1)} %broadcast_in_dim.5.base_ref), custom_call_target="tpu_custom_call" | custom-call | tf_op jit(solution)/shard_map/hazard_levels/pallas_call | solution.py:168
  137.5 0.7 copy.9
  138.1 3.3 %all-to-all-start.2 = ((f32[8,2,16]{2,1,0:T(2,128)}), f32[8,2,16]{2,1,0:T(2,128)S(1)}, u32[]{:S(2)}, u32[]{:S(2)}) async-start(f32[8,2,16]{2,1,0:T(2,128)} %bitcast.7), calls=%async_computation.2 | async-start | bytes 16384 | tf_op jit(solution)/shard_map/all_to_all | solution.py:195
  141.4 0.0 copy-done.6
  141.4 4.3 %all-to-all-done.2 = f32[8,2,16]{2,1,0:T(2,128)S(1)} async-done(((f32[8,2,16]{2,1,0:T(2,128)}), f32[8,2,16]{2,1,0:T(2,128)S(1)}, u32[]{:S(2)}, u32[]{:S(2)}) %all-to-all-start.2) | async-done | bytes 1056 | tf_op jit(solution)/shard_map/all_to_all | solution.py:195
  145.8 0.1 reshape.30
  145.9 0.6 broadcast_multiply_fusion
  (5 shorter events, 0.0 us)
Async XLA Ops:
  6.5 0.8 copy-start
  6.5 62.1 %copy-start.5 = (s32[128]{0:T(128)S(1)}, s32[128]{0:T(128)}, u32[]{:S(2)}) copy-start(s32[128]{0:T(128)} %param.10) | copy-start | bytes 1540
  6.5 120.3 %copy-start.4 = (f32[1024]{0:T(1024)S(1)}, f32[1024]{0:T(1024)}, u32[]{:S(2)}) copy-start(f32[1024]{0:T(1024)} %param.8) | copy-start | bytes 12292
  6.5 120.3 %all-gather.2.cloned.1.call-start = ((), (), s32[]{:S(2)}) async-start(), calls=%async_computation.3 | async-start | bytes 4325376 | tf_op jit(solution)/shard_map/all_gather | solution.py:189
  35.1 1.2 copy-start.2
  36.3 0.8 copy-start.3
  53.6 87.8 %copy-start.6 = (s32[128]{0:T(128)S(1)}, s32[128]{0:T(128)}, u32[]{:S(2)}) copy-start(s32[128]{0:T(128)} %param.11) | copy-start | bytes 1540
  53.6 73.2 %all-to-all-start = ((bf16[512,8,128]{2,1,0:T(8,128)(2,1)}), bf16[512,8,128]{2,1,0:T(8,128)(2,1)S(1)}, u32[]{:S(2)}, u32[]{:S(2)}) async-start(bf16[512,8,128]{2,1,0:T(8,128)(2,1)} %bitcast.1), calls=%async_computation | async-start | bytes 2097152 | tf_op jit(solution)/shard_map/all_to_all | solution.py:190
  126.9 2.2 %copy-start.1 = (bf16[16384,128]{1,0:T(8,128)(2,1)S(1)}, bf16[16384,128]{1,0:T(8,128)(2,1)}, u32[]{:S(2)}) copy-start(bf16[16384,128]{1,0:T(8,128)(2,1)} %all-gather.2.cloned.1.call-done.weights_ref) | copy-start | bytes 12582916
  138.1 7.6 %all-to-all-start.2 = ((f32[8,2,16]{2,1,0:T(2,128)}), f32[8,2,16]{2,1,0:T(2,128)S(1)}, u32[]{:S(2)}, u32[]{:S(2)}) async-start(f32[8,2,16]{2,1,0:T(2,128)} %bitcast.7), calls=%async_computation.2 | async-start | bytes 16384 | tf_op jit(solution)/shard_map/all_to_all | solution.py:195
Sparse Core Ops, SparseCore 0:
  35.2 59.2 all-gather.1

commit v2 on v1

--- a/solution.py
+++ b/solution.py
@@ -185,7 +185,7 @@
     me = lax.axis_index(("y", "c"))
     eighth = lax.dynamic_slice_in_dim(scen_weights.T, me * 128, 128, axis=1)
     shared = lax.all_to_all(jnp.broadcast_to(eighth[None], (16, 32, 128)), "z", 0, 0, tiled=True)
-    sent = gather(tile_cells, waveforms.reshape(64, C))
+    shared, sent = lax.optimization_barrier((shared, gather(tile_cells, waveforms.reshape(64, C))))
     weights = lax.all_gather(shared.reshape(512, 128), ("x", "y", "c"), axis=0, tiled=True)
     got = lax.all_to_all(sent.reshape(512, 8, 128), EVERY, 0, 0, tiled=True)
     base = lax.dynamic_slice_in_dim(level_base.astype(jnp.float32), me * 16, 16)

time: 154 us -> 149 us (0.968)
  blocking collectives: 27.6 us -> 0 us
  starting transfers between devices: 18.4 us -> 39.6 us
    all_to_all x1 -> x0, blocking collectives: 27.6 us -> none  [body(): lax.all_to_all(jnp.broadcast_to(eighth[None], (16, 32, 128)), 'z', 0, 0,...]
    all_to_all x0 -> x1, starting transfers between devices: none -> 15.7 us  [body(): lax.all_to_all(jnp.broadcast_to(eighth[None], (16, 32, 128)), 'z', 0, 0,...]
    all_to_all x1, starting transfers between devices: 15.1 us -> 20.6 us  [body(): got = lax.all_to_all(sent.reshape(512, 8, 128), EVERY, 0, 0, tiled=True)]
    unnamed x14 -> x16, local copies, waits for them, and re-layouts: 5 us -> 5.7 us
  transfers between devices with their start and end apart: 3 -> 4, of which waited for: 2 -> 2; matrix products, arithmetic and copies ran while one was open for 0% -> 0% of each run, Pallas kernels for 11% -> 11%
where the time goes in v2:
time: 149 us; the launch traced here: 148 us
  waiting for transfers between devices  62.4 us (42%)
  starting transfers between devices  39.6 us (27%)
  Pallas kernels  24.9 us (17%)
  between operations  13.5 us (9%)
  local copies, waits for them, and re-layouts  7.28 us (5%)
    all_to_all x1, waiting for transfers between devices, body(): got = lax.all_to_all(sent.reshape(512, 8, 128), EVERY, 0, 0, tiled=True)  58 us
    all_to_all x1, starting transfers between devices, body(): got = lax.all_to_all(sent.reshape(512, 8, 128), EVERY, 0, 0, tiled=True)  20.6 us
    pallas_call x1, Pallas kernels, gather(): pl.pallas_call(gather_kernel, out_shape=jax.ShapeDtypeStruct((C // 2, 128...  16.5 us
    all_to_all x1, starting transfers between devices, body(): lax.all_to_all(jnp.broadcast_to(eighth[None], (16, 32, 128)), 'z', 0, 0,...  15.7 us
    pallas_call x1, Pallas kernels, hazard_of(): pl.pallas_call(hazard_kernel, out_shape=jax.ShapeDtypeStruct((16, 128), j...  8.4 us
    unnamed x16, local copies, waits for them, and re-layouts  5.7 us
    all_to_all x1, waiting for transfers between devices, body(): lax.all_to_all(levels, ('y', 'c'), 0, 0, tiled=True).transpose(1, 0, 2)  4.34 us
    all_to_all x1, starting transfers between devices, body(): lax.all_to_all(levels, ('y', 'c'), 0, 0, tiled=True).transpose(1, 0, 2)  3.26 us
  transfers between devices with their start and end apart: 4, of which 2 were waited for; matrix products, arithmetic and copies ran while one was open for 0% of the time, Pallas kernels for 11%

profile of v2, /device:TPU:1, one launch (start us, length us, event | category | flops | bytes accessed | tf_op | source)
XLA Modules:
  0.0 148.3 jit_solution(2553161012014176552)
XLA Ops:
  6.5 0.0 copy-start
  6.5 0.0 copy-start.6
  6.5 0.0 copy-start.4
  6.5 0.8 copy-done
  7.4 0.7 broadcast_in_dim.4
  8.1 15.7 %all-to-all-start = ((bf16[16,32,128]{2,1,0:T(8,128)(2,1)}), bf16[16,32,128]{2,1,0:T(8,128)(2,1)S(1)}, u32[]{:S(2)}, u32[]{:S(2)}) async-start(bf16[16,32,128]{2,1,0:T(8,128)(2,1)} %broadcast_in_dim.4), calls=%async_computation | async-start | bytes 262144 | tf_op jit(solution)/shard_map/all_to_all | solution.py:187
  23.8 0.0 all-gather.2.cloned.1.call-start
  23.9 0.0 copy-start.2
  23.9 1.2 copy-done.2
  25.1 0.0 copy-start.3
  25.1 0.8 copy-done.3
  25.8 16.5 %gather_cells.1 = bf16[4096,128]{1,0:T(8,128)(2,1)} custom-call(s32[8192]{0:T(1024)S(1)} %copy-done.3, bf16[64,8192]{1,0:T(8,128)(2,1)S(1)} %bitcast.13), custom_call_target="tpu_custom_call" | custom-call | flops 1048576 | bytes 41943040 | tf_op jit(solution)/shard_map/gather_cells/pallas_call | solution.py:95
  42.4 0.0 copy-start.7
  42.4 0.0 all-to-all-done
  42.4 0.0 copy-start.5
  42.4 0.7 copy-done.5
  43.1 0.0 all-gather.2.cloned.1.call-update
  43.1 20.6 %all-to-all-start.1 = ((bf16[512,8,128]{2,1,0:T(8,128)(2,1)}), bf16[512,8,128]{2,1,0:T(8,128)(2,1)S(1)}, u32[]{:S(2)}, u32[]{:S(2)}) async-start(bf16[512,8,128]{2,1,0:T(8,128)(2,1)} %bitcast.2), calls=%async_computation.1 | async-start | bytes 2097152 | tf_op jit(solution)/shard_map/all_to_all | solution.py:190
  63.7 0.0 copy-done.6
  63.7 0.1 dynamic_slice.7
  63.8 58.0 %all-to-all-done.1 = bf16[512,8,128]{2,1,0:T(8,128)(2,1)S(1)} async-done(((bf16[512,8,128]{2,1,0:T(8,128)(2,1)}), bf16[512,8,128]{2,1,0:T(8,128)(2,1)S(1)}, u32[]{:S(2)}, u32[]{:S(2)}) %all-to-all-start.1) | async-done | bytes 1048608 | tf_op jit(solution)/shard_map/all_to_all | solution.py:190
  121.8 0.0 all-gather.2.cloned.1.call-done.weights_ref
  121.8 0.1 broadcast_in_dim.5.base_ref
  121.9 0.0 copy-done.4
  121.9 0.0 copy-start.1
  121.9 2.2 %copy-done.1 = bf16[16384,128]{1,0:T(8,128)(2,1)S(1)} copy-done((bf16[16384,128]{1,0:T(8,128)(2,1)S(1)}, bf16[16384,128]{1,0:T(8,128)(2,1)}, u32[]{:S(2)}) %copy-start.1) | copy-done | bytes 4194328
  124.1 8.4 %hazard_levels.1 = f32[16,128]{1,0:T(8,128)S(1)} custom-call(bf16[4096,128]{1,0:T(8,128)(2,1)S(1)} %bitcast.12, bf16[16384,128]{1,0:T(8,128)(2,1)S(1)} %copy-done.1, f32[1,1024]{1,0:T(1,128)S(1)} %bitcast.15, f32[16,128]{1,0:T(8,128)S(1)} %broadcast_in_dim.5.base_ref), custom_call_target="tpu_custom_call" | custom-call | tf_op jit(solution)/shard_map/hazard_levels/pallas_call | solution.py:168
  132.5 0.7 copy.9
  133.2 3.3 %all-to-all-start.2 = ((f32[8,2,16]{2,1,0:T(2,128)}), f32[8,2,16]{2,1,0:T(2,128)S(1)}, u32[]{:S(2)}, u32[]{:S(2)}) async-start(f32[8,2,16]{2,1,0:T(2,128)} %bitcast.7), calls=%async_computation.2 | async-start | bytes 16384 | tf_op jit(solution)/shard_map/all_to_all | solution.py:195
  136.4 0.0 copy-done.7
  136.4 4.3 %all-to-all-done.2 = f32[8,2,16]{2,1,0:T(2,128)S(1)} async-done(((f32[8,2,16]{2,1,0:T(2,128)}), f32[8,2,16]{2,1,0:T(2,128)S(1)}, u32[]{:S(2)}, u32[]{:S(2)}) %all-to-all-start.2) | async-done | bytes 1056 | tf_op jit(solution)/shard_map/all_to_all | solution.py:195
  140.8 0.1 reshape.30
  140.9 0.6 broadcast_multiply_fusion
  (4 shorter events, 0.0 us)
Async XLA Ops:
  6.5 0.8 copy-start
  6.5 57.2 %copy-start.6 = (s32[128]{0:T(128)S(1)}, s32[128]{0:T(128)}, u32[]{:S(2)}) copy-start(s32[128]{0:T(128)} %param.10) | copy-start | bytes 1540
  6.5 115.3 %copy-start.4 = (f32[1024]{0:T(1024)S(1)}, f32[1024]{0:T(1024)}, u32[]{:S(2)}) copy-start(f32[1024]{0:T(1024)} %param.8) | copy-start | bytes 12292
  8.1 34.3 %all-to-all-start = ((bf16[16,32,128]{2,1,0:T(8,128)(2,1)}), bf16[16,32,128]{2,1,0:T(8,128)(2,1)S(1)}, u32[]{:S(2)}, u32[]{:S(2)}) async-start(bf16[16,32,128]{2,1,0:T(8,128)(2,1)} %broadcast_in_dim.4), calls=%async_computation | async-start | bytes 262144 | tf_op jit(solution)/shard_map/all_to_all | solution.py:187
  23.8 98.0 %all-gather.2.cloned.1.call-start = ((), (), s32[]{:S(2)}) async-start(), calls=%async_computation.3 | async-start | bytes 4325376 | tf_op jit(solution)/shard_map/all_gather | solution.py:189
  23.9 1.2 copy-start.2
  25.1 0.8 copy-start.3
  42.4 94.0 %copy-start.7 = (s32[128]{0:T(128)S(1)}, s32[128]{0:T(128)}, u32[]{:S(2)}) copy-start(s32[128]{0:T(128)} %param.11) | copy-start | bytes 1540
  42.4 0.7 copy-start.5
  43.1 78.7 %all-to-all-start.1 = ((bf16[512,8,128]{2,1,0:T(8,128)(2,1)}), bf16[512,8,128]{2,1,0:T(8,128)(2,1)S(1)}, u32[]{:S(2)}, u32[]{:S(2)}) async-start(bf16[512,8,128]{2,1,0:T(8,128)(2,1)} %bitcast.2), calls=%async_computation.1 | async-start | bytes 2097152 | tf_op jit(solution)/shard_map/all_to_all | solution.py:190
  121.9 2.2 %copy-start.1 = (bf16[16384,128]{1,0:T(8,128)(2,1)S(1)}, bf16[16384,128]{1,0:T(8,128)(2,1)}, u32[]{:S(2)}) copy-start(bf16[16384,128]{1,0:T(8,128)(2,1)} %all-gather.2.cloned.1.call-done.weights_ref) | copy-start | bytes 12582916
  133.2 7.6 %all-to-all-start.2 = ((f32[8,2,16]{2,1,0:T(2,128)}), f32[8,2,16]{2,1,0:T(2,128)S(1)}, u32[]{:S(2)}, u32[]{:S(2)}) async-start(f32[8,2,16]{2,1,0:T(2,128)} %bitcast.7), calls=%async_computation.2 | async-start | bytes 16384 | tf_op jit(solution)/shard_map/all_to_all | solution.py:195
Sparse Core Ops, SparseCore 0:
  43.2 65.2 all-gather.1

commit v3 on v2

v3 whole, which is shorter than its diff:
```python
import functools

import jax
import jax.numpy as jnp
from jax import lax
from jax.experimental import pallas as pl
from jax.experimental.pallas import tpu as pltpu
from jax.sharding import Mesh, PartitionSpec as P

K = 1024
NB = 16
C = 8192
EVERY = ("z", "x", "y", "c")
MIB = 1 << 20

ERFC = (
    0.17087277,
    -0.82215223,
    1.48851587,
    -1.13520398,
    0.27886807,
    -0.18628806,
    0.09678418,
    0.37409196,
    1.00002368,
    -1.26551223,
)


def erfc(x):
    size = jnp.abs(x)
    t = 1.0 / (1.0 + 0.5 * size)
    total = jnp.full_like(t, ERFC[0])
    for c in ERFC[1:]:
        total = total * t + c
    tail = t * jnp.exp(total - x * x)
    return jnp.where(x < 0.0, 2.0 - tail, tail)


def gather_kernel(cells_ref, wave_ref, out_ref, turned, picked):
    half = C // 2

    @pl.loop(0, half // 128)
    def _(j):
        low = wave_ref[:, pl.ds(pl.multiple_of(j * 128, 128), 128)]
        high = wave_ref[:, pl.ds(pl.multiple_of(half + j * 128, 128), 128)]
        one = jnp.concatenate([low, high], axis=0).T.astype(jnp.float32)
        two = jnp.concatenate([high, low], axis=0).T.astype(jnp.float32)
        turned[pl.ds(pl.multiple_of(j * 128, 128), 128), :] = one
        turned[pl.ds(pl.multiple_of(half + j * 128, 128), 128), :] = two
        turned[pl.ds(pl.multiple_of(C + j * 128, 128), 128), :] = one

    first = lax.broadcasted_iota(jnp.int32, (1, 128), 1) < 64

    @pl.loop(0, C // 64)
    def _(four):
        for e in range(4):
            for a in range(8):
                at = four * 64 + e * 16 + a
                one = turned[pl.ds(cells_ref[at], 1), :]
                two = turned[pl.ds(cells_ref[at + 8] + half, 1), :]
                picked[pl.ds(four * 32 + e * 8 + a, 1), :] = jnp.where(first, one, two)

    @pl.loop(0, C // 2 // 128)
    def _(i):
        rows = pl.ds(pl.multiple_of(i * 128, 128), 128)
        out_ref[rows, :] = picked[rows, :].astype(jnp.bfloat16)


def gather(cells, wave):
    return pl.pallas_call(
        gather_kernel,
        out_shape=jax.ShapeDtypeStruct((C // 2, 128), jnp.bfloat16),
        in_specs=[pl.BlockSpec(memory_space=pltpu.SMEM), pl.BlockSpec(memory_space=pltpu.VMEM)],
        out_specs=pl.BlockSpec(memory_space=pltpu.VMEM),
        scratch_shapes=[pltpu.VMEM((C + C // 2, 128), jnp.float32), pltpu.VMEM((C // 2, 128), jnp.float32)],
        compiler_params=pltpu.CompilerParams(vmem_limit_bytes=60 * MIB),
        cost_estimate=pl.CostEstimate(flops=1 << 20, bytes_accessed=40 * MIB, transcendentals=0),
        name="gather_cells",
    )(cells, wave)


def hazard_kernel(me_ref, got_ref, weights_ref, rates_ref, base_ref, wet_ref, out_ref, columns, weights, logs, sums, sem):
    copy = pltpu.make_async_copy(weights_ref, weights, sem)
    copy.start()
    scale = 1.0 / (0.5 * jnp.sqrt(jnp.float32(2.0)))
    lane = lax.broadcasted_iota(jnp.int32, (16, 128), 1)
    in64 = lane < 64
    in32 = (lane & 63) < 32

    def swap(one, two, shift, mask):
        return (
            jnp.where(mask, one, pltpu.roll(two, shift, 1)),
            jnp.where(mask, pltpu.roll(one, 128 - shift, 1), two),
        )

    @pl.loop(0, 4)
    def _(x):
        for y in range(4):
            for zq in range(4):
                tiles = []
                for i in range(4):
                    row = (4 * zq + i) * 256 + x * 64 + y * 16
                    tiles.append(got_ref[pl.ds(pl.multiple_of(row, 16), 16), :].astype(jnp.float32))
                v0, v2 = swap(tiles[0], tiles[2], 64, in64)
                v1, v3 = swap(tiles[1], tiles[3], 64, in64)
                w0, w1 = swap(v0, v1, 32, in32)
                w2, w3 = swap(v2, v3, 32, in32)
                for c in range(2):
                    part = slice(8 * c, 8 * c + 8)
                    for t, (early, late) in enumerate(((w0, w2), (w1, w3))):
                        block = jnp.concatenate([early[part], late[part]], axis=0)
                        at = ((2 * y + c) * 2 + t) * 16
                        columns[at : at + 16, pl.ds(pl.multiple_of(x * 512 + zq * 128, 128), 128)] = block.astype(jnp.bfloat16)

    copy.wait()
    for n in range(4):
        total = jnp.zeros((256, 256), jnp.float32)
        for x in range(4):
            at = (x * 8 + 2 * n) * 512
            right = jnp.concatenate([weights[at : at + 512, :], weights[at + 512 : at + 1024, :]], axis=1)
            total += jnp.dot(columns[:, x * 512 : (x + 1) * 512], right, preferred_element_type=jnp.float32)
        peak = total[0:16]
        for t in range(1, 16):
            peak = jnp.maximum(peak, total[t * 16 : (t + 1) * 16])
        logs[:, n * 256 : (n + 1) * 256] = jnp.log(jnp.maximum(peak, 0.1))

    row = lax.broadcasted_iota(jnp.int32, (16, 128), 0)
    mine = lane == me_ref[0] * 16 + row
    base = jnp.sum(jnp.where(mine, base_ref[...].astype(jnp.float32), 0.0), axis=1, keepdims=True)
    wet = wet_ref[...].astype(jnp.float32)
    bottom = jnp.log(jnp.full((16, 1), 0.1, jnp.float32))

    @pl.loop(0, NB)
    def _(j):
        log_level = jnp.broadcast_to(bottom + 0.15 * (base + j.astype(jnp.float32)), (16, 128))
        total = jnp.zeros((16, 128), jnp.float32)
        for b in range(8):
            part = slice(b * 128, b * 128 + 128)
            total += rates_ref[:, part] * erfc((log_level - logs[:, part]) * scale)
        sums[pl.ds(pl.multiple_of(j * 16, 16), 16), :] = total

    for j in range(NB):
        hazard = jnp.sum(sums[j * 16 : j * 16 + 16, :], axis=1, keepdims=True) * (0.5 / K)
        out_ref[j : j + 1, :] = jnp.sum(jnp.where(mine, hazard, 0.0), axis=0, keepdims=True) * wet


def hazard_of(me, got, weights, rates, base, wet):
    vmem = pl.BlockSpec(memory_space=pltpu.VMEM)
    return pl.pallas_call(
        hazard_kernel,
        out_shape=jax.ShapeDtypeStruct((16, 128), jnp.float32),
        in_specs=[pl.BlockSpec(memory_space=pltpu.SMEM), vmem, pl.BlockSpec(memory_space=pl.ANY), vmem, vmem, vmem],
        out_specs=vmem,
        scratch_shapes=[
            pltpu.VMEM((256, 2048), jnp.bfloat16),
            pltpu.VMEM((16384, 128), jnp.bfloat16),
            pltpu.VMEM((16, 1024), jnp.float32),
            pltpu.VMEM((256, 128), jnp.float32),
            pltpu.SemaphoreType.DMA,
        ],
        compiler_params=pltpu.CompilerParams(vmem_limit_bytes=58 * MIB),
        name="hazard_levels",
    )(me, got, weights, rates, base, wet)


def body(waveforms, scen_weights, rates, tile_cells, level_base, wet_mask):
    me = lax.axis_index(("y", "c"))
    eighth = lax.dynamic_slice_in_dim(scen_weights.T, me * 128, 128, axis=1)
    shared = lax.all_to_all(jnp.broadcast_to(eighth[None], (16, 32, 128)), "z", 0, 0, tiled=True)
    shared, sent = lax.optimization_barrier((shared, gather(tile_cells, waveforms.reshape(64, C))))
    weights = lax.all_gather(shared.reshape(512, 128), ("x", "y", "c"), axis=0, tiled=True)
    got = lax.all_to_all(sent.reshape(512, 8, 128), EVERY, 0, 0, tiled=True)
    part = hazard_of(
        me.reshape(1),
        got.reshape(C // 2, 128),
        weights,
        rates.reshape(1, K),
        level_base.reshape(1, 128),
        wet_mask.reshape(1, 128),
    )
    hazard = lax.all_to_all(part.reshape(8, 2, 128), ("y", "c"), 0, 0, tiled=True)
    return jnp.sum(hazard, axis=0)


def solution(mesh):
    split = Mesh(mesh.devices.reshape(16, 4, 4, 2), EVERY)
    src, tm = ("z", "x"), ("y", "c")
    return jax.shard_map(
        body,
        mesh=split,
        in_specs=(P(tm, src, None), P(None, src), P(), P(), P(src), P(src)),
        out_specs=P(tm, src),
        check_vma=False,
    )
```

time: 149 us -> 138 us (0.926)
  blocking collectives: 0 us -> 86.5 us
  waiting for transfers between devices: 62.4 us -> 0.02 us
  starting transfers between devices: 39.6 us -> 15.8 us
  Pallas kernels: 24.9 us -> 18.9 us
  local copies, waits for them, and re-layouts: 7.28 us -> 2.17 us
    all_to_all x0 -> x2, blocking collectives: none -> 86.5 us  [the longest x1 78.8 us: body(): got = lax.all_to_all(sent.reshape(512, 8, 128), EVERY, 0, 0, tiled=True)]
    all_to_all x2 -> x0, waiting for transfers between devices: 62.4 us -> none  [the longest x1 58 us: body(): got = lax.all_to_all(sent.reshape(512, 8, 128), EVERY, 0, 0, tiled=True)]
    all_to_all x2 -> x0, starting transfers between devices: 23.8 us -> none  [the longest x1 20.6 us: body(): got = lax.all_to_all(sent.reshape(512, 8, 128), EVERY, 0, 0, tiled=True)]
    pallas_call x1, Pallas kernels: 16.5 us -> 12 us  [gather(): pl.pallas_call(gather_kernel, out_shape=jax.ShapeDtypeStruct((C // 2, 128...]
    unnamed x16 -> x4, local copies, waits for them, and re-layouts: 5.7 us -> 1.49 us
  transfers between devices with their start and end apart: 4 -> 2, of which waited for: 2 -> 0; matrix products, arithmetic and copies ran while one was open for 0% -> 0% of each run, Pallas kernels for 11% -> 9%
where the time goes in v3:
time: 138 us; the launch traced here: 137 us
  blocking collectives  86.5 us (63%)
  Pallas kernels  18.9 us (14%)
  starting transfers between devices  15.8 us (11%)
  between operations  13.4 us (10%)
  local copies, waits for them, and re-layouts  2.17 us (2%)
    all_to_all x1, blocking collectives, body(): got = lax.all_to_all(sent.reshape(512, 8, 128), EVERY, 0, 0, tiled=True)  78.8 us
    all_to_all x1, starting transfers between devices, body(): lax.all_to_all(jnp.broadcast_to(eighth[None], (16, 32, 128)), 'z', 0, 0,...  15.7 us
    pallas_call x1, Pallas kernels, gather(): pl.pallas_call(gather_kernel, out_shape=jax.ShapeDtypeStruct((C // 2, 128...  12 us
    all_to_all x1, blocking collectives, body(): lax.all_to_all(part.reshape(8, 2, 128), ('y', 'c'), 0, 0, tiled=True)  7.64 us
    pallas_call x1, Pallas kernels, hazard_of(): pl.pallas_call(hazard_kernel, out_shape=jax.ShapeDtypeStruct((16, 128), j...  6.97 us
  transfers between devices with their start and end apart: 2, of which 0 were waited for; matrix products, arithmetic and copies ran while one was open for 0% of the time, Pallas kernels for 9%

profile of v3, /device:TPU:1, one launch (start us, length us, event | category | flops | bytes accessed | tf_op | source)
XLA Modules:
  0.0 137.4 jit_solution(12463944079914730135)
XLA Ops:
  6.5 0.0 copy-start
  6.5 0.8 copy-done
  7.4 0.7 broadcast_in_dim.2
  8.1 15.7 %all-to-all-start = ((bf16[16,32,128]{2,1,0:T(8,128)(2,1)}), bf16[16,32,128]{2,1,0:T(8,128)(2,1)S(1)}, u32[]{:S(2)}, u32[]{:S(2)}) async-start(bf16[16,32,128]{2,1,0:T(8,128)(2,1)} %broadcast_in_dim.2), calls=%async_computation | async-start | bytes 262144 | tf_op jit(solution)/shard_map/all_to_all | solution.py:170
  23.8 0.0 all-gather.2.cloned.1.call-start
  23.9 12.0 %gather_cells.1 = bf16[4096,128]{1,0:T(8,128)(2,1)} custom-call(s32[8192]{0:T(1024)} %cells_ref.1, bf16[64,8192]{1,0:T(8,128)(2,1)} %bitcast.13), custom_call_target="tpu_custom_call" | custom-call | flops 1048576 | bytes 41943040 | tf_op jit(solution)/shard_map/gather_cells/pallas_call | solution.py:71
  35.8 0.0 all-to-all-done
  35.8 0.0 copy-start.1
  35.8 0.7 copy-done.1
  36.5 0.0 all-gather.2.cloned.1.call-update
  36.5 78.8 %all_to_all.15 = bf16[512,8,128]{2,1,0:T(8,128)(2,1)} all-to-all(bf16[512,8,128]{2,1,0:T(8,128)(2,1)} %bitcast.11), channel_id=1, replica_groups=mesh['z'=16,'x'=4,'y'=4,'c'=2] {'z','x','y','c'}, dimensions={0} | all-to-all | bytes 2097152 | tf_op jit(solution)/shard_map/all_to_all | solution.py:173
  115.3 0.0 all-gather.2.cloned.1.call-done.weights_ref
  115.3 7.0 %hazard_levels.1 = f32[16,128]{1,0:T(8,128)} custom-call(s32[1]{0:T(128)} %bitcast.me_ref, bf16[4096,128]{1,0:T(8,128)(2,1)} %bitcast.12, bf16[16384,128]{1,0:T(8,128)(2,1)} %all-gather.2.cloned.1.call-done.weights_ref, f32[1,1024]{1,0:T(1,128)} %bitcast.16, s32[1,128]{1,0:T(1,128)} %bitcast.17, s32[1,128]{1,0:T(1,128)} %bitcast.18), custom_call_target="tpu_custom_call" | custom-call | tf_op jit(solution)/shard_map/hazard_levels/pallas_call | solution.py:150
  122.3 7.6 %all_to_all.16 = f32[8,2,128]{2,1,0:T(2,128)S(1)} all-to-all(f32[8,2,128]{2,1,0:T(2,128)} %bitcast.15), channel_id=1, replica_groups=mesh['z'=16,'x'=4,'y'=4,'c'=2] {'y','c'}, dimensions={0} | all-to-all | bytes 16384 | tf_op jit(solution)/shard_map/all_to_all | solution.py:182
  130.0 0.6 reduce_sum.9
  (1 shorter events, 0.0 us)
Async XLA Ops:
  6.5 0.8 copy-start
  8.1 27.8 %all-to-all-start = ((bf16[16,32,128]{2,1,0:T(8,128)(2,1)}), bf16[16,32,128]{2,1,0:T(8,128)(2,1)S(1)}, u32[]{:S(2)}, u32[]{:S(2)}) async-start(bf16[16,32,128]{2,1,0:T(8,128)(2,1)} %broadcast_in_dim.2), calls=%async_computation | async-start | bytes 262144 | tf_op jit(solution)/shard_map/all_to_all | solution.py:170
  23.8 91.5 %all-gather.2.cloned.1.call-start = ((), (), s32[]{:S(2)}) async-start(), calls=%async_computation.3 | async-start | bytes 4325376 | tf_op jit(solution)/shard_map/all_gather | solution.py:172
  35.8 0.7 copy-start.1
Sparse Core Ops, SparseCore 0:
  36.6 65.1 all-gather.1

commit v4 on v3

v4 whole, which is shorter than its diff:
```python
import functools

import jax
import jax.numpy as jnp
from jax import lax
from jax.experimental import pallas as pl
from jax.experimental.pallas import tpu as pltpu
from jax.sharding import Mesh, PartitionSpec as P

K = 1024
NB = 16
C = 8192
EVERY = ("z", "x", "y", "c")
MIB = 1 << 20
NEAR = (0, 1, 15, 2, 14, 3, 13, 4)
FAR = (12, 5, 11, 6, 10, 7, 9, 8)

ERFC = (
    0.17087277,
    -0.82215223,
    1.48851587,
    -1.13520398,
    0.27886807,
    -0.18628806,
    0.09678418,
    0.37409196,
    1.00002368,
    -1.26551223,
)


def erfc(x):
    size = jnp.abs(x)
    t = 1.0 / (1.0 + 0.5 * size)
    total = jnp.full_like(t, ERFC[0])
    for c in ERFC[1:]:
        total = total * t + c
    tail = t * jnp.exp(total - x * x)
    return jnp.where(x < 0.0, 2.0 - tail, tail)


def gather_kernel(cells_hbm, wave_hbm, out_hbm, cells, wave, turned, picked, out, cells_sem, wave_sem, out_sem):
    half, part = C // 2, C // 8
    cells_copy = pltpu.make_async_copy(cells_hbm, cells, cells_sem)
    loads = []
    for k in range(4):
        for h in range(2):
            lanes = slice(h * half + k * part, h * half + (k + 1) * part)
            loads.append(pltpu.make_async_copy(wave_hbm.at[:, lanes], wave.at[:, lanes], wave_sem.at[2 * k + h]))
    for copy in loads[:2] + [cells_copy] + loads[2:]:
        copy.start()

    for k in range(4):
        loads[2 * k].wait()
        loads[2 * k + 1].wait()

        @pl.loop(k * part // 128, (k + 1) * part // 128)
        def _(j):
            low = wave[:, pl.ds(pl.multiple_of(j * 128, 128), 128)]
            high = wave[:, pl.ds(pl.multiple_of(half + j * 128, 128), 128)]
            one = jnp.concatenate([low, high], axis=0).T.astype(jnp.float32)
            two = jnp.concatenate([high, low], axis=0).T.astype(jnp.float32)
            turned[pl.ds(pl.multiple_of(j * 128, 128), 128), :] = one
            turned[pl.ds(pl.multiple_of(half + j * 128, 128), 128), :] = two
            turned[pl.ds(pl.multiple_of(C + j * 128, 128), 128), :] = one

    cells_copy.wait()
    first = lax.broadcasted_iota(jnp.int32, (1, 128), 1) < 64
    stores = []
    for k in range(4):

        @pl.loop(k * C // 256, (k + 1) * C // 256)
        def _(four):
            for e in range(4):
                for a in range(8):
                    at = four * 64 + e * 16 + a
                    one = turned[pl.ds(cells[at], 1), :]
                    two = turned[pl.ds(cells[at + 8] + half, 1), :]
                    picked[pl.ds(four * 32 + e * 8 + a, 1), :] = jnp.where(first, one, two)

        @pl.loop(k * part // 128, (k + 1) * part // 128)
        def _(i):
            rows = pl.ds(pl.multiple_of(i * 128, 128), 128)
            out[rows, :] = picked[rows, :].astype(jnp.bfloat16)

        rows = slice(k * part, (k + 1) * part)
        stores.append(pltpu.make_async_copy(out.at[rows], out_hbm.at[rows], out_sem.at[k]))
        stores[k].start()
    for copy in stores:
        copy.wait()


def gather(cells, wave):
    hbm = pl.BlockSpec(memory_space=pl.ANY)
    return pl.pallas_call(
        gather_kernel,
        out_shape=jax.ShapeDtypeStruct((C // 2, 128), jnp.bfloat16),
        in_specs=[hbm, hbm],
        out_specs=hbm,
        scratch_shapes=[
            pltpu.SMEM((C,), jnp.int32),
            pltpu.VMEM((64, C), jnp.bfloat16),
            pltpu.VMEM((C + C // 2, 128), jnp.float32),
            pltpu.VMEM((C // 2, 128), jnp.float32),
            pltpu.VMEM((C // 2, 128), jnp.bfloat16),
            pltpu.SemaphoreType.DMA,
            pltpu.SemaphoreType.DMA((8,)),
            pltpu.SemaphoreType.DMA((4,)),
        ],
        compiler_params=pltpu.CompilerParams(vmem_limit_bytes=60 * MIB),
        cost_estimate=pl.CostEstimate(flops=1 << 20, bytes_accessed=40 * MIB, transcendentals=0),
        name="gather_cells",
    )(cells, wave)


def hazard_kernel(me_ref, got_ref, weights_ref, rates_ref, base_ref, wet_ref, out_ref, columns, weights, logs, sums, sem):
    copy = pltpu.make_async_copy(weights_ref, weights, sem)
    copy.start()
    scale = 1.0 / (0.5 * jnp.sqrt(jnp.float32(2.0)))
    lane = lax.broadcasted_iota(jnp.int32, (16, 128), 1)
    starts = []
    for near, far in zip(NEAR, FAR):
        for ahead in (near, far):
            starts.append(((me_ref[1] + ahead) & 15) * 256)

    to = lax.broadcasted_iota(jnp.int32, (1, 512), 1)
    source = ((to >> 5) & 3) * 128 + (to >> 7) * 32 + (to & 31)
    swap = (lax.broadcasted_iota(jnp.int32, (512, 512), 0) == source).astype(jnp.float32).astype(jnp.bfloat16)

    for x in range(4):
        tiles = []
        for y in range(4):
            for zq in range(4):
                rows = [pl.ds(pl.multiple_of(starts[4 * zq + i] + x * 64 + y * 16, 16), 16) for i in range(4)]
                tiles.append(jnp.concatenate([got_ref[row, :] for row in rows], axis=1))
        moved = jnp.dot(jnp.concatenate(tiles, axis=0), swap, preferred_element_type=jnp.float32)
        for y in range(4):
            for zq in range(4):
                at = (y * 4 + zq) * 16
                lanes = slice(x * 512 + zq * 128, x * 512 + zq * 128 + 128)
                for c in range(2):
                    part = moved[at + 8 * c : at + 8 * c + 8]
                    for t in range(2):
                        early, late = part[:, t * 128 : t * 128 + 128], part[:, 256 + t * 128 : 384 + t * 128]
                        to_row = ((2 * y + c) * 2 + t) * 16
                        columns[to_row : to_row + 16, lanes] = jnp.concatenate([early, late], axis=0).astype(jnp.bfloat16)

    copy.wait()
    for n in range(4):
        total = jnp.dot(columns[...], weights[:, n * 256 : (n + 1) * 256], preferred_element_type=jnp.float32)
        peak = total[0:16]
        for t in range(1, 16):
            peak = jnp.maximum(peak, total[t * 16 : (t + 1) * 16])
        logs[:, n * 256 : (n + 1) * 256] = jnp.log(jnp.maximum(peak, 0.1))

    row = lax.broadcasted_iota(jnp.int32, (16, 128), 0)
    mine = lane == me_ref[0] * 16 + row
    base = jnp.sum(jnp.where(mine, base_ref[...].astype(jnp.float32), 0.0), axis=1, keepdims=True)
    wet = wet_ref[...].astype(jnp.float32)
    bottom = jnp.log(jnp.full((16, 1), 0.1, jnp.float32))

    @pl.loop(0, NB)
    def _(j):
        log_level = jnp.broadcast_to(bottom + 0.15 * (base + j.astype(jnp.float32)), (16, 128))
        total = jnp.zeros((16, 128), jnp.float32)
        for b in range(8):
            part = slice(b * 128, b * 128 + 128)
            total += rates_ref[:, part] * erfc((log_level - logs[:, part]) * scale)
        sums[pl.ds(pl.multiple_of(j * 16, 16), 16), :] = total

    for j in range(NB):
        hazard = jnp.sum(sums[j * 16 : j * 16 + 16, :], axis=1, keepdims=True) * (0.5 / K)
        out_ref[j : j + 1, :] = jnp.sum(jnp.where(mine, hazard, 0.0), axis=0, keepdims=True) * wet


def hazard_of(me, got, weights, rates, base, wet):
    vmem = pl.BlockSpec(memory_space=pltpu.VMEM)
    return pl.pallas_call(
        hazard_kernel,
        out_shape=jax.ShapeDtypeStruct((16, 128), jnp.float32),
        in_specs=[pl.BlockSpec(memory_space=pltpu.SMEM), vmem, pl.BlockSpec(memory_space=pl.ANY), vmem, vmem, vmem],
        out_specs=vmem,
        scratch_shapes=[
            pltpu.VMEM((256, 2048), jnp.bfloat16),
            pltpu.VMEM((2048, K), jnp.bfloat16),
            pltpu.VMEM((16, 1024), jnp.float32),
            pltpu.VMEM((256, 128), jnp.float32),
            pltpu.SemaphoreType.DMA,
        ],
        compiler_params=pltpu.CompilerParams(vmem_limit_bytes=52 * MIB),
        name="hazard_levels",
    )(me, got, weights, rates, base, wet)


def body(waveforms, scen_weights, rates, tile_cells, level_base, wet_mask):
    me, z = lax.axis_index(("y", "c")), lax.axis_index("z")

    def fetch(steps):
        ring = [(((i + steps[r]) % 16) * 8 + r, i * 8 + r) for i in range(16) for r in range(8)]
        return lax.ppermute(scen_weights.T, ("z", "y", "c"), ring)

    far, near = fetch(FAR), fetch(NEAR)
    far, near, sent = lax.optimization_barrier((far, near, gather(tile_cells, waveforms.reshape(64, C))))
    weights = lax.all_gather(jnp.concatenate([near, far], axis=0), ("x", "y", "c"), axis=0, tiled=True)
    got = lax.all_to_all(sent.reshape(512, 8, 128), EVERY, 0, 0, tiled=True)
    part = hazard_of(
        jnp.stack([me, z]),
        got.reshape(C // 2, 128),
        weights,
        rates.reshape(1, K),
        level_base.reshape(1, 128),
        wet_mask.reshape(1, 128),
    )
    hazard = lax.all_to_all(part.reshape(8, 2, 128), ("y", "c"), 0, 0, tiled=True)
    return jnp.sum(hazard, axis=0)


def solution(mesh):
    split = Mesh(mesh.devices.reshape(16, 4, 4, 2), EVERY)
    src, tm = ("z", "x"), ("y", "c")
    return jax.shard_map(
        body,
        mesh=split,
        in_specs=(P(tm, src, None), P(None, src), P(), P(), P(src), P(src)),
        out_specs=P(tm, src),
        check_vma=False,
    )
```

time: 138 us -> 133 us (0.964)
  blocking collectives: 86.5 us -> 7.54 us
  waiting for transfers between devices: 0.02 us -> 58 us
  starting transfers between devices: 15.8 us -> 34.7 us
  local copies, waits for them, and re-layouts: 2.17 us -> 0.01 us
    all_to_all x1 -> x0, blocking collectives: 78.8 us -> none  [body(): got = lax.all_to_all(sent.reshape(512, 8, 128), EVERY, 0, 0, tiled=True)]
    all_to_all x1, waiting for transfers between devices: 0.01 us -> 57.9 us  [body(): got = lax.all_to_all(sent.reshape(512, 8, 128), EVERY, 0, 0, tiled=True)]
    ppermute x0 -> x2, starting transfers between devices: none -> 17.7 us  [fetch(): return lax.ppermute(scen_weights.T, ('z', 'y', 'c'), ring)]
    unnamed x4 -> x6, local copies, waits for them, and re-layouts: 1.49 us -> 0.01 us
  transfers between devices with their start and end apart: 2 -> 4, of which waited for: 0 -> 1; matrix products, arithmetic and copies ran while one was open for 0% -> 0% of each run, Pallas kernels for 9% -> 9%
where the time goes in v4:
time: 133 us
  waiting for transfers between devices  58 us (44%)
  starting transfers between devices  34.7 us (26%)
  Pallas kernels  17.8 us (13%)
  between operations  13.5 us (10%)
  blocking collectives  7.54 us (6%)
    all_to_all x1, waiting for transfers between devices, body(): got = lax.all_to_all(sent.reshape(512, 8, 128), EVERY, 0, 0, tiled=True)  57.9 us
    ppermute x2, starting transfers between devices, fetch(): return lax.ppermute(scen_weights.T, ('z', 'y', 'c'), ring)  17.7 us
    all_to_all x1, starting transfers between devices, body(): got = lax.all_to_all(sent.reshape(512, 8, 128), EVERY, 0, 0, tiled=True)  17 us
    pallas_call x1, Pallas kernels, gather(): pl.pallas_call(gather_kernel, out_shape=jax.ShapeDtypeStruct((C // 2, 128...  11.6 us
    all_to_all x1, blocking collectives, body(): lax.all_to_all(part.reshape(8, 2, 128), ('y', 'c'), 0, 0, tiled=True)  7.54 us
    pallas_call x1, Pallas kernels, hazard_of(): pl.pallas_call(hazard_kernel, out_shape=jax.ShapeDtypeStruct((16, 128), j...  6.25 us
  transfers between devices with their start and end apart: 4, of which 1 were waited for; matrix products, arithmetic and copies ran while one was open for 0% of the time, Pallas kernels for 9%

profile of v4, /device:TPU:1, one launch (start us, length us, event | category | flops | bytes accessed | tf_op | source)
XLA Modules:
  0.0 132.8 jit_solution(311840951428614067)
XLA Ops:
  6.5 0.0 copy-start.2
  6.5 0.0 copy-start.1
  6.5 0.0 copy-start
  6.5 0.0 all-gather.2.cloned.1.call-start
  6.5 12.1 %collective-permute-start.1 = (bf16[32,1024]{1,0:T(8,128)(2,1)}, bf16[32,1024]{1,0:T(8,128)(2,1)S(1)}, u32[]{:S(2)}, u32[]{:S(2)}) collective-permute-start(bf16[32,1024]{1,0:T(8,128)(2,1)} %bitcast.17), channel_id=1, source_target_pairs={{0,0},{33,1},{482,2},{67,3},{452,4},{101,5},{422,6},{135,7},{32,32... | collective-permute-start | bytes 196616 | tf_op jit(solution)/shard_map/ppermute | solution.py:200
  18.6 5.6 %collective-permute-start = (bf16[32,1024]{1,0:T(8,128)(2,1)}, bf16[32,1024]{1,0:T(8,128)(2,1)S(1)}, u32[]{:S(2)}, u32[]{:S(2)}) collective-permute-start(bf16[32,1024]{1,0:T(8,128)(2,1)} %bitcast.18), channel_id=1, source_target_pairs={{384,0},{161,1},{354,2},{195,3},{324,4},{229,5},{294,6},{263,7},{4... | collective-permute-start | bytes 196616 | tf_op jit(solution)/shard_map/ppermute | solution.py:200
  24.3 11.6 %gather_cells.1 = bf16[4096,128]{1,0:T(8,128)(2,1)} custom-call(s32[8192]{0:T(1024)} %cells_hbm.1, bf16[64,8192]{1,0:T(8,128)(2,1)} %bitcast.16), custom_call_target="tpu_custom_call" | custom-call | flops 1048576 | bytes 41943040 | tf_op jit(solution)/shard_map/gather_cells/pallas_call | solution.py:95
  35.8 0.0 collective-permute-done.1
  35.9 0.0 collective-permute-done
  35.9 0.7 pad_maximum_fusion
  36.5 0.0 all-gather.2.cloned.1.call-update
  36.6 17.0 %all-to-all-start = ((bf16[512,8,128]{2,1,0:T(8,128)(2,1)}), bf16[512,8,128]{2,1,0:T(8,128)(2,1)S(1)}, u32[]{:S(2)}, u32[]{:S(2)}) async-start(bf16[512,8,128]{2,1,0:T(8,128)(2,1)} %bitcast.15), calls=%async_computation | async-start | bytes 2097152 | tf_op jit(solution)/shard_map/all_to_all | solution.py:205
  53.6 0.1 pad_add_fusion.me_ref
  53.7 57.9 %all-to-all-done = bf16[512,8,128]{2,1,0:T(8,128)(2,1)S(1)} async-done(((bf16[512,8,128]{2,1,0:T(8,128)(2,1)}), bf16[512,8,128]{2,1,0:T(8,128)(2,1)S(1)}, u32[]{:S(2)}, u32[]{:S(2)}) %all-to-all-start) | async-done | bytes 1048608 | tf_op jit(solution)/shard_map/all_to_all | solution.py:205
  111.6 0.0 all-gather.2.cloned.1.call-done.weights_ref
  111.6 0.0 copy-done.2
  111.6 0.0 copy-done.1
  111.6 0.0 copy-done
  111.6 6.3 %hazard_levels.1 = f32[16,128]{1,0:T(8,128)S(1)} custom-call(s32[2]{0:T(128)S(1)} %pad_add_fusion.me_ref, bf16[4096,128]{1,0:T(8,128)(2,1)S(1)} %bitcast.10, bf16[2048,1024]{1,0:T(8,128)(2,1)} %all-gather.2.cloned.1.call-done.weights_ref, f32[1,1024]{1,0:T(1,128)S(1)} %bitcast.12, s32[1,128]{1,0:T(1,128)S(1)} %bitcast.13, s32[1,128]{1,0:T(1,128)S(1)} %bitcast.14), custom_call_target="tpu_custom_call" | custom-call | tf_op jit(solution)/shard_map/hazard_levels/pallas_call | solution.py:178
  117.9 7.5 %all_to_all.10 = f32[8,2,128]{2,1,0:T(2,128)S(1)} all-to-all(f32[8,2,128]{2,1,0:T(2,128)S(1)} %bitcast.11), channel_id=1, replica_groups=mesh['z'=16,'x'=4,'y'=4,'c'=2] {'y','c'}, dimensions={0} | all-to-all | bytes 16384 | tf_op jit(solution)/shard_map/all_to_all | solution.py:214
  125.4 0.6 reduce_sum.9
Async XLA Ops:
  6.5 105.1 %copy-start.2 = (s32[128]{0:T(128)S(1)}, s32[128]{0:T(128)}, u32[]{:S(2)}) copy-start(s32[128]{0:T(128)} %param.11) | copy-start | bytes 1540
  6.5 105.1 %copy-start.1 = (s32[128]{0:T(128)S(1)}, s32[128]{0:T(128)}, u32[]{:S(2)}) copy-start(s32[128]{0:T(128)} %param.10) | copy-start | bytes 1540
  6.5 105.1 %copy-start = (f32[1024]{0:T(1024)S(1)}, f32[1024]{0:T(1024)}, u32[]{:S(2)}) copy-start(f32[1024]{0:T(1024)} %param.8) | copy-start | bytes 12292
  6.5 105.1 %all-gather.2.cloned.1.call-start = ((), (), s32[]{:S(2)}) async-start(), calls=%async_computation.2 | async-start | bytes 4325376 | tf_op jit(solution)/shard_map/all_gather | solution.py:204
  6.5 29.3 %collective-permute-start.1 = (bf16[32,1024]{1,0:T(8,128)(2,1)}, bf16[32,1024]{1,0:T(8,128)(2,1)S(1)}, u32[]{:S(2)}, u32[]{:S(2)}) collective-permute-start(bf16[32,1024]{1,0:T(8,128)(2,1)} %bitcast.17), channel_id=1, source_target_pairs={{0,0},{33,1},{482,2},{67,3},{452,4},{101,5},{422,6},{135,7},{32,32... | collective-permute-start | bytes 196616 | tf_op jit(solution)/shard_map/ppermute | solution.py:200
  18.6 17.2 %collective-permute-start = (bf16[32,1024]{1,0:T(8,128)(2,1)}, bf16[32,1024]{1,0:T(8,128)(2,1)S(1)}, u32[]{:S(2)}, u32[]{:S(2)}) collective-permute-start(bf16[32,1024]{1,0:T(8,128)(2,1)} %bitcast.18), channel_id=1, source_target_pairs={{384,0},{161,1},{354,2},{195,3},{324,4},{229,5},{294,6},{263,7},{4... | collective-permute-start | bytes 196616 | tf_op jit(solution)/shard_map/ppermute | solution.py:200
  36.6 75.0 %all-to-all-start = ((bf16[512,8,128]{2,1,0:T(8,128)(2,1)}), bf16[512,8,128]{2,1,0:T(8,128)(2,1)S(1)}, u32[]{:S(2)}, u32[]{:S(2)}) async-start(bf16[512,8,128]{2,1,0:T(8,128)(2,1)} %bitcast.15), calls=%async_computation | async-start | bytes 2097152 | tf_op jit(solution)/shard_map/all_to_all | solution.py:205
Sparse Core Ops, SparseCore 0:
  36.7 61.6 all-gather.1

commit v5 on v4

--- a/solution.py
+++ b/solution.py
@@ -120,7 +120,7 @@
     lane = lax.broadcasted_iota(jnp.int32, (16, 128), 1)
     starts = []
     for near, far in zip(NEAR, FAR):
-        for ahead in (near, far):
+        for ahead in (far, near):
             starts.append(((me_ref[1] + ahead) & 15) * 256)
 
     to = lax.broadcasted_iota(jnp.int32, (1, 512), 1)
@@ -199,9 +199,9 @@
         ring = [(((i + steps[r]) % 16) * 8 + r, i * 8 + r) for i in range(16) for r in range(8)]
         return lax.ppermute(scen_weights.T, ("z", "y", "c"), ring)
 
-    far, near = fetch(FAR), fetch(NEAR)
-    far, near, sent = lax.optimization_barrier((far, near, gather(tile_cells, waveforms.reshape(64, C))))
-    weights = lax.all_gather(jnp.concatenate([near, far], axis=0), ("x", "y", "c"), axis=0, tiled=True)
+    near, far = fetch(NEAR), fetch(FAR)
+    near, far, sent = lax.optimization_barrier((near, far, gather(tile_cells, waveforms.reshape(64, C))))
+    weights = lax.all_gather(jnp.concatenate([far, near], axis=0), ("x", "y", "c"), axis=0, tiled=True)
     got = lax.all_to_all(sent.reshape(512, 8, 128), EVERY, 0, 0, tiled=True)
     part = hazard_of(
         jnp.stack([me, z]),

time: 133 us -> 133 us (level)
  no operation moved by 1% of the time
where the time goes in v5:
time: 133 us
  waiting for transfers between devices  58 us (44%)
  starting transfers between devices  34.7 us (26%)
  Pallas kernels  17.8 us (13%)
  between operations  13.5 us (10%)
  blocking collectives  7.54 us (6%)
    all_to_all x1, waiting for transfers between devices, body(): got = lax.all_to_all(sent.reshape(512, 8, 128), EVERY, 0, 0, tiled=True)  57.9 us
    ppermute x2, starting transfers between devices, fetch(): return lax.ppermute(scen_weights.T, ('z', 'y', 'c'), ring)  17.7 us
    all_to_all x1, starting transfers between devices, body(): got = lax.all_to_all(sent.reshape(512, 8, 128), EVERY, 0, 0, tiled=True)  17 us
    pallas_call x1, Pallas kernels, gather(): pl.pallas_call(gather_kernel, out_shape=jax.ShapeDtypeStruct((C // 2, 128...  11.6 us
    all_to_all x1, blocking collectives, body(): lax.all_to_all(part.reshape(8, 2, 128), ('y', 'c'), 0, 0, tiled=True)  7.54 us
    pallas_call x1, Pallas kernels, hazard_of(): pl.pallas_call(hazard_kernel, out_shape=jax.ShapeDtypeStruct((16, 128), j...  6.25 us
  transfers between devices with their start and end apart: 4, of which 1 were waited for; matrix products, arithmetic and copies ran while one was open for 0% of the time, Pallas kernels for 9%

profile of v5, /device:TPU:1, one launch (start us, length us, event | category | flops | bytes accessed | tf_op | source)
XLA Modules:
  0.0 132.8 jit_solution(10506421912752070491)
XLA Ops:
  6.5 0.0 copy-start.2
  6.5 0.0 copy-start.1
  6.5 0.0 copy-start
  6.5 0.0 all-gather.2.cloned.1.call-start
  6.5 15.1 %collective-permute-start.1 = (bf16[32,1024]{1,0:T(8,128)(2,1)}, bf16[32,1024]{1,0:T(8,128)(2,1)S(1)}, u32[]{:S(2)}, u32[]{:S(2)}) collective-permute-start(bf16[32,1024]{1,0:T(8,128)(2,1)} %bitcast.17), channel_id=1, source_target_pairs={{384,0},{161,1},{354,2},{195,3},{324,4},{229,5},{294,6},{263,7},{4... | collective-permute-start | bytes 196616 | tf_op jit(solution)/shard_map/ppermute | solution.py:200
  21.6 2.6 %collective-permute-start = (bf16[32,1024]{1,0:T(8,128)(2,1)}, bf16[32,1024]{1,0:T(8,128)(2,1)S(1)}, u32[]{:S(2)}, u32[]{:S(2)}) collective-permute-start(bf16[32,1024]{1,0:T(8,128)(2,1)} %bitcast.18), channel_id=1, source_target_pairs={{0,0},{33,1},{482,2},{67,3},{452,4},{101,5},{422,6},{135,7},{32,32... | collective-permute-start | bytes 196616 | tf_op jit(solution)/shard_map/ppermute | solution.py:200
  24.3 11.6 %gather_cells.1 = bf16[4096,128]{1,0:T(8,128)(2,1)} custom-call(s32[8192]{0:T(1024)} %cells_hbm.1, bf16[64,8192]{1,0:T(8,128)(2,1)} %bitcast.16), custom_call_target="tpu_custom_call" | custom-call | flops 1048576 | bytes 41943040 | tf_op jit(solution)/shard_map/gather_cells/pallas_call | solution.py:95
  35.8 0.0 collective-permute-done.1
  35.9 0.0 collective-permute-done
  35.9 0.7 pad_maximum_fusion
  36.5 0.0 all-gather.2.cloned.1.call-update
  36.6 17.0 %all-to-all-start = ((bf16[512,8,128]{2,1,0:T(8,128)(2,1)}), bf16[512,8,128]{2,1,0:T(8,128)(2,1)S(1)}, u32[]{:S(2)}, u32[]{:S(2)}) async-start(bf16[512,8,128]{2,1,0:T(8,128)(2,1)} %bitcast.15), calls=%async_computation | async-start | bytes 2097152 | tf_op jit(solution)/shard_map/all_to_all | solution.py:205
  53.6 0.1 pad_add_fusion.me_ref
  53.7 57.9 %all-to-all-done = bf16[512,8,128]{2,1,0:T(8,128)(2,1)S(1)} async-done(((bf16[512,8,128]{2,1,0:T(8,128)(2,1)}), bf16[512,8,128]{2,1,0:T(8,128)(2,1)S(1)}, u32[]{:S(2)}, u32[]{:S(2)}) %all-to-all-start) | async-done | bytes 1048608 | tf_op jit(solution)/shard_map/all_to_all | solution.py:205
  111.6 0.0 all-gather.2.cloned.1.call-done.weights_ref
  111.6 0.0 copy-done.2
  111.6 0.0 copy-done.1
  111.6 0.0 copy-done
  111.6 6.3 %hazard_levels.1 = f32[16,128]{1,0:T(8,128)S(1)} custom-call(s32[2]{0:T(128)S(1)} %pad_add_fusion.me_ref, bf16[4096,128]{1,0:T(8,128)(2,1)S(1)} %bitcast.10, bf16[2048,1024]{1,0:T(8,128)(2,1)} %all-gather.2.cloned.1.call-done.weights_ref, f32[1,1024]{1,0:T(1,128)S(1)} %bitcast.12, s32[1,128]{1,0:T(1,128)S(1)} %bitcast.13, s32[1,128]{1,0:T(1,128)S(1)} %bitcast.14), custom_call_target="tpu_custom_call" | custom-call | tf_op jit(solution)/shard_map/hazard_levels/pallas_call | solution.py:178
  117.9 7.5 %all_to_all.10 = f32[8,2,128]{2,1,0:T(2,128)S(1)} all-to-all(f32[8,2,128]{2,1,0:T(2,128)S(1)} %bitcast.11), channel_id=1, replica_groups=mesh['z'=16,'x'=4,'y'=4,'c'=2] {'y','c'}, dimensions={0} | all-to-all | bytes 16384 | tf_op jit(solution)/shard_map/all_to_all | solution.py:214
  125.4 0.6 reduce_sum.9
Async XLA Ops:
  6.5 105.1 %copy-start.2 = (s32[128]{0:T(128)S(1)}, s32[128]{0:T(128)}, u32[]{:S(2)}) copy-start(s32[128]{0:T(128)} %param.11) | copy-start | bytes 1540
  6.5 105.1 %copy-start.1 = (s32[128]{0:T(128)S(1)}, s32[128]{0:T(128)}, u32[]{:S(2)}) copy-start(s32[128]{0:T(128)} %param.10) | copy-start | bytes 1540
  6.5 105.1 %copy-start = (f32[1024]{0:T(1024)S(1)}, f32[1024]{0:T(1024)}, u32[]{:S(2)}) copy-start(f32[1024]{0:T(1024)} %param.8) | copy-start | bytes 12292
  6.5 105.1 %all-gather.2.cloned.1.call-start = ((), (), s32[]{:S(2)}) async-start(), calls=%async_computation.2 | async-start | bytes 4325376 | tf_op jit(solution)/shard_map/all_gather | solution.py:204
  6.5 29.3 %collective-permute-start.1 = (bf16[32,1024]{1,0:T(8,128)(2,1)}, bf16[32,1024]{1,0:T(8,128)(2,1)S(1)}, u32[]{:S(2)}, u32[]{:S(2)}) collective-permute-start(bf16[32,1024]{1,0:T(8,128)(2,1)} %bitcast.17), channel_id=1, source_target_pairs={{384,0},{161,1},{354,2},{195,3},{324,4},{229,5},{294,6},{263,7},{4... | collective-permute-start | bytes 196616 | tf_op jit(solution)/shard_map/ppermute | solution.py:200
  21.6 14.2 %collective-permute-start = (bf16[32,1024]{1,0:T(8,128)(2,1)}, bf16[32,1024]{1,0:T(8,128)(2,1)S(1)}, u32[]{:S(2)}, u32[]{:S(2)}) collective-permute-start(bf16[32,1024]{1,0:T(8,128)(2,1)} %bitcast.18), channel_id=1, source_target_pairs={{0,0},{33,1},{482,2},{67,3},{452,4},{101,5},{422,6},{135,7},{32,32... | collective-permute-start | bytes 196616 | tf_op jit(solution)/shard_map/ppermute | solution.py:200
  36.6 75.0 %all-to-all-start = ((bf16[512,8,128]{2,1,0:T(8,128)(2,1)}), bf16[512,8,128]{2,1,0:T(8,128)(2,1)S(1)}, u32[]{:S(2)}, u32[]{:S(2)}) async-start(bf16[512,8,128]{2,1,0:T(8,128)(2,1)} %bitcast.15), calls=%async_computation | async-start | bytes 2097152 | tf_op jit(solution)/shard_map/all_to_all | solution.py:205
Sparse Core Ops, SparseCore 0:
  36.7 61.6 all-gather.1

commit v6 on v4

--- a/solution.py
+++ b/solution.py
@@ -13,7 +13,7 @@
 EVERY = ("z", "x", "y", "c")
 MIB = 1 << 20
 NEAR = (0, 1, 15, 2, 14, 3, 13, 4)
-FAR = (12, 5, 11, 6, 10, 7, 9, 8)
+FAR = (8, 7, 9, 6, 10, 5, 11, 12)
 
 ERFC = (
     0.17087277,

time: 133 us -> 131 us (0.985)
  starting transfers between devices: 34.7 us -> 33 us
    all_to_all x1, starting transfers between devices: 17 us -> 14.4 us  [body(): got = lax.all_to_all(sent.reshape(512, 8, 128), EVERY, 0, 0, tiled=True)]
where the time goes in v6:
time: 131 us
  waiting for transfers between devices  58.1 us (44%)
  starting transfers between devices  33 us (25%)
  Pallas kernels  17.8 us (14%)
  between operations  13.5 us (10%)
  blocking collectives  7.43 us (6%)
  other arithmetic  1.32 us (1%)
    all_to_all x1, waiting for transfers between devices, body(): got = lax.all_to_all(sent.reshape(512, 8, 128), EVERY, 0, 0, tiled=True)  58 us
    ppermute x2, starting transfers between devices, fetch(): return lax.ppermute(scen_weights.T, ('z', 'y', 'c'), ring)  18.6 us
    all_to_all x1, starting transfers between devices, body(): got = lax.all_to_all(sent.reshape(512, 8, 128), EVERY, 0, 0, tiled=True)  14.4 us
    pallas_call x1, Pallas kernels, gather(): pl.pallas_call(gather_kernel, out_shape=jax.ShapeDtypeStruct((C // 2, 128...  11.6 us
    all_to_all x1, blocking collectives, body(): lax.all_to_all(part.reshape(8, 2, 128), ('y', 'c'), 0, 0, tiled=True)  7.43 us
    pallas_call x1, Pallas kernels, hazard_of(): pl.pallas_call(hazard_kernel, out_shape=jax.ShapeDtypeStruct((16, 128), j...  6.26 us
  transfers between devices with their start and end apart: 4, of which 1 were waited for; matrix products, arithmetic and copies ran while one was open for 0% of the time, Pallas kernels for 9%

profile of v6, /device:TPU:1, one launch (start us, length us, event | category | flops | bytes accessed | tf_op | source)
XLA Modules:
  0.0 131.1 jit_solution(3200810610247180492)
XLA Ops:
  6.5 0.0 copy-start.2
  6.5 0.0 copy-start.1
  6.5 0.0 copy-start
  6.5 0.0 all-gather.2.cloned.1.call-start
  6.5 12.1 %collective-permute-start.1 = (bf16[32,1024]{1,0:T(8,128)(2,1)}, bf16[32,1024]{1,0:T(8,128)(2,1)S(1)}, u32[]{:S(2)}, u32[]{:S(2)}) collective-permute-start(bf16[32,1024]{1,0:T(8,128)(2,1)} %bitcast.17), channel_id=1, source_target_pairs={{0,0},{33,1},{482,2},{67,3},{452,4},{101,5},{422,6},{135,7},{32,32... | collective-permute-start | bytes 196616 | tf_op jit(solution)/shard_map/ppermute | solution.py:200
  18.6 6.5 %collective-permute-start = (bf16[32,1024]{1,0:T(8,128)(2,1)}, bf16[32,1024]{1,0:T(8,128)(2,1)S(1)}, u32[]{:S(2)}, u32[]{:S(2)}) collective-permute-start(bf16[32,1024]{1,0:T(8,128)(2,1)} %bitcast.18), channel_id=1, source_target_pairs={{256,0},{225,1},{290,2},{195,3},{324,4},{165,5},{358,6},{391,7},{2... | collective-permute-start | bytes 196616 | tf_op jit(solution)/shard_map/ppermute | solution.py:200
  25.1 11.6 %gather_cells.1 = bf16[4096,128]{1,0:T(8,128)(2,1)} custom-call(s32[8192]{0:T(1024)} %cells_hbm.1, bf16[64,8192]{1,0:T(8,128)(2,1)} %bitcast.16), custom_call_target="tpu_custom_call" | custom-call | flops 1048576 | bytes 41943040 | tf_op jit(solution)/shard_map/gather_cells/pallas_call | solution.py:95
  36.7 0.0 collective-permute-done.1
  36.7 0.0 collective-permute-done
  36.8 0.7 pad_maximum_fusion
  37.4 0.0 all-gather.2.cloned.1.call-update
  37.4 14.4 %all-to-all-start = ((bf16[512,8,128]{2,1,0:T(8,128)(2,1)}), bf16[512,8,128]{2,1,0:T(8,128)(2,1)S(1)}, u32[]{:S(2)}, u32[]{:S(2)}) async-start(bf16[512,8,128]{2,1,0:T(8,128)(2,1)} %bitcast.15), calls=%async_computation | async-start | bytes 2097152 | tf_op jit(solution)/shard_map/all_to_all | solution.py:205
  51.8 0.1 pad_add_fusion.me_ref
  51.9 58.0 %all-to-all-done = bf16[512,8,128]{2,1,0:T(8,128)(2,1)S(1)} async-done(((bf16[512,8,128]{2,1,0:T(8,128)(2,1)}), bf16[512,8,128]{2,1,0:T(8,128)(2,1)S(1)}, u32[]{:S(2)}, u32[]{:S(2)}) %all-to-all-start) | async-done | bytes 1048608 | tf_op jit(solution)/shard_map/all_to_all | solution.py:205
  109.9 0.0 all-gather.2.cloned.1.call-done.weights_ref
  109.9 0.0 copy-done.2
  109.9 0.0 copy-done.1
  109.9 0.0 copy-done
  110.0 6.3 %hazard_levels.1 = f32[16,128]{1,0:T(8,128)S(1)} custom-call(s32[2]{0:T(128)S(1)} %pad_add_fusion.me_ref, bf16[4096,128]{1,0:T(8,128)(2,1)S(1)} %bitcast.10, bf16[2048,1024]{1,0:T(8,128)(2,1)} %all-gather.2.cloned.1.call-done.weights_ref, f32[1,1024]{1,0:T(1,128)S(1)} %bitcast.12, s32[1,128]{1,0:T(1,128)S(1)} %bitcast.13, s32[1,128]{1,0:T(1,128)S(1)} %bitcast.14), custom_call_target="tpu_custom_call" | custom-call | tf_op jit(solution)/shard_map/hazard_levels/pallas_call | solution.py:178
  116.2 7.4 %all_to_all.10 = f32[8,2,128]{2,1,0:T(2,128)S(1)} all-to-all(f32[8,2,128]{2,1,0:T(2,128)S(1)} %bitcast.11), channel_id=1, replica_groups=mesh['z'=16,'x'=4,'y'=4,'c'=2] {'y','c'}, dimensions={0} | all-to-all | bytes 16384 | tf_op jit(solution)/shard_map/all_to_all | solution.py:214
  123.6 0.6 reduce_sum.9
Async XLA Ops:
  6.5 103.4 %copy-start.2 = (s32[128]{0:T(128)S(1)}, s32[128]{0:T(128)}, u32[]{:S(2)}) copy-start(s32[128]{0:T(128)} %param.11) | copy-start | bytes 1540
  6.5 103.4 %copy-start.1 = (s32[128]{0:T(128)S(1)}, s32[128]{0:T(128)}, u32[]{:S(2)}) copy-start(s32[128]{0:T(128)} %param.10) | copy-start | bytes 1540
  6.5 103.4 %copy-start = (f32[1024]{0:T(1024)S(1)}, f32[1024]{0:T(1024)}, u32[]{:S(2)}) copy-start(f32[1024]{0:T(1024)} %param.8) | copy-start | bytes 12292
  6.5 103.4 %all-gather.2.cloned.1.call-start = ((), (), s32[]{:S(2)}) async-start(), calls=%async_computation.2 | async-start | bytes 4325376 | tf_op jit(solution)/shard_map/all_gather | solution.py:204
  6.5 30.2 %collective-permute-start.1 = (bf16[32,1024]{1,0:T(8,128)(2,1)}, bf16[32,1024]{1,0:T(8,128)(2,1)S(1)}, u32[]{:S(2)}, u32[]{:S(2)}) collective-permute-start(bf16[32,1024]{1,0:T(8,128)(2,1)} %bitcast.17), channel_id=1, source_target_pairs={{0,0},{33,1},{482,2},{67,3},{452,4},{101,5},{422,6},{135,7},{32,32... | collective-permute-start | bytes 196616 | tf_op jit(solution)/shard_map/ppermute | solution.py:200
  18.6 18.1 %collective-permute-start = (bf16[32,1024]{1,0:T(8,128)(2,1)}, bf16[32,1024]{1,0:T(8,128)(2,1)S(1)}, u32[]{:S(2)}, u32[]{:S(2)}) collective-permute-start(bf16[32,1024]{1,0:T(8,128)(2,1)} %bitcast.18), channel_id=1, source_target_pairs={{256,0},{225,1},{290,2},{195,3},{324,4},{165,5},{358,6},{391,7},{2... | collective-permute-start | bytes 196616 | tf_op jit(solution)/shard_map/ppermute | solution.py:200
  37.4 72.5 %all-to-all-start = ((bf16[512,8,128]{2,1,0:T(8,128)(2,1)}), bf16[512,8,128]{2,1,0:T(8,128)(2,1)S(1)}, u32[]{:S(2)}, u32[]{:S(2)}) async-start(bf16[512,8,128]{2,1,0:T(8,128)(2,1)} %bitcast.15), calls=%async_computation | async-start | bytes 2097152 | tf_op jit(solution)/shard_map/all_to_all | solution.py:205
Sparse Core Ops, SparseCore 0:
  37.6 59.0 all-gather.1

commit v7 on v5

--- a/solution.py
+++ b/solution.py
@@ -13,7 +13,7 @@
 EVERY = ("z", "x", "y", "c")
 MIB = 1 << 20
 NEAR = (0, 1, 15, 2, 14, 3, 13, 4)
-FAR = (12, 5, 11, 6, 10, 7, 9, 8)
+FAR = (8, 7, 9, 6, 10, 5, 11, 12)
 
 ERFC = (
     0.17087277,

time: 133 us -> 131 us (0.985)
  starting transfers between devices: 34.7 us -> 32.9 us
    all_to_all x1, starting transfers between devices: 17 us -> 14.3 us  [body(): got = lax.all_to_all(sent.reshape(512, 8, 128), EVERY, 0, 0, tiled=True)]
where the time goes in v7:
time: 131 us
  waiting for transfers between devices  58 us (44%)
  starting transfers between devices  32.9 us (25%)
  Pallas kernels  17.8 us (14%)
  between operations  13.5 us (10%)
  blocking collectives  7.54 us (6%)
  other arithmetic  1.32 us (1%)
    all_to_all x1, waiting for transfers between devices, body(): got = lax.all_to_all(sent.reshape(512, 8, 128), EVERY, 0, 0, tiled=True)  57.9 us
    ppermute x2, starting transfers between devices, fetch(): return lax.ppermute(scen_weights.T, ('z', 'y', 'c'), ring)  18.6 us
    all_to_all x1, starting transfers between devices, body(): got = lax.all_to_all(sent.reshape(512, 8, 128), EVERY, 0, 0, tiled=True)  14.3 us
    pallas_call x1, Pallas kernels, gather(): pl.pallas_call(gather_kernel, out_shape=jax.ShapeDtypeStruct((C // 2, 128...  11.6 us
    all_to_all x1, blocking collectives, body(): lax.all_to_all(part.reshape(8, 2, 128), ('y', 'c'), 0, 0, tiled=True)  7.54 us
    pallas_call x1, Pallas kernels, hazard_of(): pl.pallas_call(hazard_kernel, out_shape=jax.ShapeDtypeStruct((16, 128), j...  6.25 us
  transfers between devices with their start and end apart: 4, of which 1 were waited for; matrix products, arithmetic and copies ran while one was open for 0% of the time, Pallas kernels for 9%

profile of v7, /device:TPU:1, one launch (start us, length us, event | category | flops | bytes accessed | tf_op | source)
XLA Modules:
  0.0 131.0 jit_solution(17940276688627390954)
XLA Ops:
  6.5 0.0 copy-start.2
  6.5 0.0 copy-start.1
  6.5 0.0 copy-start
  6.5 0.0 all-gather.2.cloned.1.call-start
  6.5 16.0 %collective-permute-start.1 = (bf16[32,1024]{1,0:T(8,128)(2,1)}, bf16[32,1024]{1,0:T(8,128)(2,1)S(1)}, u32[]{:S(2)}, u32[]{:S(2)}) collective-permute-start(bf16[32,1024]{1,0:T(8,128)(2,1)} %bitcast.17), channel_id=1, source_target_pairs={{256,0},{225,1},{290,2},{195,3},{324,4},{165,5},{358,6},{391,7},{2... | collective-permute-start | bytes 196616 | tf_op jit(solution)/shard_map/ppermute | solution.py:200
  22.5 2.6 %collective-permute-start = (bf16[32,1024]{1,0:T(8,128)(2,1)}, bf16[32,1024]{1,0:T(8,128)(2,1)S(1)}, u32[]{:S(2)}, u32[]{:S(2)}) collective-permute-start(bf16[32,1024]{1,0:T(8,128)(2,1)} %bitcast.18), channel_id=1, source_target_pairs={{0,0},{33,1},{482,2},{67,3},{452,4},{101,5},{422,6},{135,7},{32,32... | collective-permute-start | bytes 196616 | tf_op jit(solution)/shard_map/ppermute | solution.py:200
  25.1 11.6 %gather_cells.1 = bf16[4096,128]{1,0:T(8,128)(2,1)} custom-call(s32[8192]{0:T(1024)} %cells_hbm.1, bf16[64,8192]{1,0:T(8,128)(2,1)} %bitcast.16), custom_call_target="tpu_custom_call" | custom-call | flops 1048576 | bytes 41943040 | tf_op jit(solution)/shard_map/gather_cells/pallas_call | solution.py:95
  36.7 0.0 collective-permute-done.1
  36.7 0.0 collective-permute-done
  36.8 0.7 pad_maximum_fusion
  37.4 0.0 all-gather.2.cloned.1.call-update
  37.4 14.3 %all-to-all-start = ((bf16[512,8,128]{2,1,0:T(8,128)(2,1)}), bf16[512,8,128]{2,1,0:T(8,128)(2,1)S(1)}, u32[]{:S(2)}, u32[]{:S(2)}) async-start(bf16[512,8,128]{2,1,0:T(8,128)(2,1)} %bitcast.15), calls=%async_computation | async-start | bytes 2097152 | tf_op jit(solution)/shard_map/all_to_all | solution.py:205
  51.8 0.1 pad_add_fusion.me_ref
  51.8 57.9 %all-to-all-done = bf16[512,8,128]{2,1,0:T(8,128)(2,1)S(1)} async-done(((bf16[512,8,128]{2,1,0:T(8,128)(2,1)}), bf16[512,8,128]{2,1,0:T(8,128)(2,1)S(1)}, u32[]{:S(2)}, u32[]{:S(2)}) %all-to-all-start) | async-done | bytes 1048608 | tf_op jit(solution)/shard_map/all_to_all | solution.py:205
  109.8 0.0 all-gather.2.cloned.1.call-done.weights_ref
  109.8 0.0 copy-done.2
  109.8 0.0 copy-done.1
  109.8 0.0 copy-done
  109.8 6.3 %hazard_levels.1 = f32[16,128]{1,0:T(8,128)S(1)} custom-call(s32[2]{0:T(128)S(1)} %pad_add_fusion.me_ref, bf16[4096,128]{1,0:T(8,128)(2,1)S(1)} %bitcast.10, bf16[2048,1024]{1,0:T(8,128)(2,1)} %all-gather.2.cloned.1.call-done.weights_ref, f32[1,1024]{1,0:T(1,128)S(1)} %bitcast.12, s32[1,128]{1,0:T(1,128)S(1)} %bitcast.13, s32[1,128]{1,0:T(1,128)S(1)} %bitcast.14), custom_call_target="tpu_custom_call" | custom-call | tf_op jit(solution)/shard_map/hazard_levels/pallas_call | solution.py:178
  116.1 7.5 %all_to_all.10 = f32[8,2,128]{2,1,0:T(2,128)S(1)} all-to-all(f32[8,2,128]{2,1,0:T(2,128)S(1)} %bitcast.11), channel_id=1, replica_groups=mesh['z'=16,'x'=4,'y'=4,'c'=2] {'y','c'}, dimensions={0} | all-to-all | bytes 16384 | tf_op jit(solution)/shard_map/all_to_all | solution.py:214
  123.6 0.6 reduce_sum.9
Async XLA Ops:
  6.5 103.2 %copy-start.2 = (s32[128]{0:T(128)S(1)}, s32[128]{0:T(128)}, u32[]{:S(2)}) copy-start(s32[128]{0:T(128)} %param.11) | copy-start | bytes 1540
  6.5 103.3 %copy-start.1 = (s32[128]{0:T(128)S(1)}, s32[128]{0:T(128)}, u32[]{:S(2)}) copy-start(s32[128]{0:T(128)} %param.10) | copy-start | bytes 1540
  6.5 103.3 %copy-start = (f32[1024]{0:T(1024)S(1)}, f32[1024]{0:T(1024)}, u32[]{:S(2)}) copy-start(f32[1024]{0:T(1024)} %param.8) | copy-start | bytes 12292
  6.5 103.2 %all-gather.2.cloned.1.call-start = ((), (), s32[]{:S(2)}) async-start(), calls=%async_computation.2 | async-start | bytes 4325376 | tf_op jit(solution)/shard_map/all_gather | solution.py:204
  6.5 30.2 %collective-permute-start.1 = (bf16[32,1024]{1,0:T(8,128)(2,1)}, bf16[32,1024]{1,0:T(8,128)(2,1)S(1)}, u32[]{:S(2)}, u32[]{:S(2)}) collective-permute-start(bf16[32,1024]{1,0:T(8,128)(2,1)} %bitcast.17), channel_id=1, source_target_pairs={{256,0},{225,1},{290,2},{195,3},{324,4},{165,5},{358,6},{391,7},{2... | collective-permute-start | bytes 196616 | tf_op jit(solution)/shard_map/ppermute | solution.py:200
  22.5 14.2 %collective-permute-start = (bf16[32,1024]{1,0:T(8,128)(2,1)}, bf16[32,1024]{1,0:T(8,128)(2,1)S(1)}, u32[]{:S(2)}, u32[]{:S(2)}) collective-permute-start(bf16[32,1024]{1,0:T(8,128)(2,1)} %bitcast.18), channel_id=1, source_target_pairs={{0,0},{33,1},{482,2},{67,3},{452,4},{101,5},{422,6},{135,7},{32,32... | collective-permute-start | bytes 196616 | tf_op jit(solution)/shard_map/ppermute | solution.py:200
  37.4 72.3 %all-to-all-start = ((bf16[512,8,128]{2,1,0:T(8,128)(2,1)}), bf16[512,8,128]{2,1,0:T(8,128)(2,1)S(1)}, u32[]{:S(2)}, u32[]{:S(2)}) async-start(bf16[512,8,128]{2,1,0:T(8,128)(2,1)} %bitcast.15), calls=%async_computation | async-start | bytes 2097152 | tf_op jit(solution)/shard_map/all_to_all | solution.py:205
Sparse Core Ops, SparseCore 0:
  37.6 58.9 all-gather.1

commit v8 on v6

--- a/solution.py
+++ b/solution.py
@@ -13,7 +13,7 @@
 EVERY = ("z", "x", "y", "c")
 MIB = 1 << 20
 NEAR = (0, 1, 15, 2, 14, 3, 13, 4)
-FAR = (8, 7, 9, 6, 10, 5, 11, 12)
+FAR = (8, 9, 7, 10, 6, 11, 5, 12)
 
 ERFC = (
     0.17087277,
@@ -159,7 +159,7 @@
     wet = wet_ref[...].astype(jnp.float32)
     bottom = jnp.log(jnp.full((16, 1), 0.1, jnp.float32))
 
-    @pl.loop(0, NB)
+    @pl.loop(0, NB, unroll=4)
     def _(j):
         log_level = jnp.broadcast_to(bottom + 0.15 * (base + j.astype(jnp.float32)), (16, 128))
         total = jnp.zeros((16, 128), jnp.float32)

time: 131 us -> 131 us (level)
    all_to_all x1, starting transfers between devices: 14.4 us -> 17.4 us  [body(): got = lax.all_to_all(sent.reshape(512, 8, 128), EVERY, 0, 0, tiled=True)]
    ppermute x2, starting transfers between devices: 18.6 us -> 15.8 us  [fetch(): return lax.ppermute(scen_weights.T, ('z', 'y', 'c'), ring)]
where the time goes in v8:
time: 131 us
  waiting for transfers between devices  58.1 us (44%)
  starting transfers between devices  33.1 us (25%)
  Pallas kernels  17.5 us (13%)
  between operations  13.5 us (10%)
  blocking collectives  7.43 us (6%)
  other arithmetic  1.32 us (1%)
    all_to_all x1, waiting for transfers between devices, body(): got = lax.all_to_all(sent.reshape(512, 8, 128), EVERY, 0, 0, tiled=True)  58 us
    all_to_all x1, starting transfers between devices, body(): got = lax.all_to_all(sent.reshape(512, 8, 128), EVERY, 0, 0, tiled=True)  17.4 us
    ppermute x2, starting transfers between devices, fetch(): return lax.ppermute(scen_weights.T, ('z', 'y', 'c'), ring)  15.8 us
    pallas_call x1, Pallas kernels, gather(): pl.pallas_call(gather_kernel, out_shape=jax.ShapeDtypeStruct((C // 2, 128...  11.6 us
    all_to_all x1, blocking collectives, body(): lax.all_to_all(part.reshape(8, 2, 128), ('y', 'c'), 0, 0, tiled=True)  7.43 us
    pallas_call x1, Pallas kernels, hazard_of(): pl.pallas_call(hazard_kernel, out_shape=jax.ShapeDtypeStruct((16, 128), j...  5.96 us
  transfers between devices with their start and end apart: 4, of which 1 were waited for; matrix products, arithmetic and copies ran while one was open for 0% of the time, Pallas kernels for 9%

profile of v8, /device:TPU:1, one launch (start us, length us, event | category | flops | bytes accessed | tf_op | source)
XLA Modules:
  0.0 130.9 jit_solution(6217743949727621680)
XLA Ops:
  6.5 0.0 copy-start.2
  6.5 0.0 copy-start.1
  6.5 0.0 copy-start
  6.5 0.0 all-gather.2.cloned.1.call-start
  6.5 12.1 %collective-permute-start.1 = (bf16[32,1024]{1,0:T(8,128)(2,1)}, bf16[32,1024]{1,0:T(8,128)(2,1)S(1)}, u32[]{:S(2)}, u32[]{:S(2)}) collective-permute-start(bf16[32,1024]{1,0:T(8,128)(2,1)} %bitcast.17), channel_id=1, source_target_pairs={{0,0},{33,1},{482,2},{67,3},{452,4},{101,5},{422,6},{135,7},{32,32... | collective-permute-start | bytes 196616 | tf_op jit(solution)/shard_map/ppermute | solution.py:200
  18.6 3.7 %collective-permute-start = (bf16[32,1024]{1,0:T(8,128)(2,1)}, bf16[32,1024]{1,0:T(8,128)(2,1)S(1)}, u32[]{:S(2)}, u32[]{:S(2)}) collective-permute-start(bf16[32,1024]{1,0:T(8,128)(2,1)} %bitcast.18), channel_id=1, source_target_pairs={{256,0},{289,1},{226,2},{323,3},{196,4},{357,5},{166,6},{391,7},{2... | collective-permute-start | bytes 196616 | tf_op jit(solution)/shard_map/ppermute | solution.py:200
  22.3 11.6 %gather_cells.1 = bf16[4096,128]{1,0:T(8,128)(2,1)} custom-call(s32[8192]{0:T(1024)} %cells_hbm.1, bf16[64,8192]{1,0:T(8,128)(2,1)} %bitcast.16), custom_call_target="tpu_custom_call" | custom-call | flops 1048576 | bytes 41943040 | tf_op jit(solution)/shard_map/gather_cells/pallas_call | solution.py:95
  33.9 0.0 collective-permute-done.1
  33.9 0.0 collective-permute-done
  33.9 0.7 pad_maximum_fusion
  34.6 0.0 all-gather.2.cloned.1.call-update
  34.6 17.4 %all-to-all-start = ((bf16[512,8,128]{2,1,0:T(8,128)(2,1)}), bf16[512,8,128]{2,1,0:T(8,128)(2,1)S(1)}, u32[]{:S(2)}, u32[]{:S(2)}) async-start(bf16[512,8,128]{2,1,0:T(8,128)(2,1)} %bitcast.15), calls=%async_computation | async-start | bytes 2097152 | tf_op jit(solution)/shard_map/all_to_all | solution.py:205
  52.0 0.1 pad_add_fusion.me_ref
  52.1 58.0 %all-to-all-done = bf16[512,8,128]{2,1,0:T(8,128)(2,1)S(1)} async-done(((bf16[512,8,128]{2,1,0:T(8,128)(2,1)}), bf16[512,8,128]{2,1,0:T(8,128)(2,1)S(1)}, u32[]{:S(2)}, u32[]{:S(2)}) %all-to-all-start) | async-done | bytes 1048608 | tf_op jit(solution)/shard_map/all_to_all | solution.py:205
  110.1 0.0 all-gather.2.cloned.1.call-done.weights_ref
  110.1 0.0 copy-done.2
  110.1 0.0 copy-done.1
  110.1 0.0 copy-done
  110.1 6.0 %hazard_levels.1 = f32[16,128]{1,0:T(8,128)S(1)} custom-call(s32[2]{0:T(128)S(1)} %pad_add_fusion.me_ref, bf16[4096,128]{1,0:T(8,128)(2,1)S(1)} %bitcast.10, bf16[2048,1024]{1,0:T(8,128)(2,1)} %all-gather.2.cloned.1.call-done.weights_ref, f32[1,1024]{1,0:T(1,128)S(1)} %bitcast.12, s32[1,128]{1,0:T(1,128)S(1)} %bitcast.13, s32[1,128]{1,0:T(1,128)S(1)} %bitcast.14), custom_call_target="tpu_custom_call" | custom-call | tf_op jit(solution)/shard_map/hazard_levels/pallas_call | solution.py:178
  116.1 7.4 %all_to_all.10 = f32[8,2,128]{2,1,0:T(2,128)S(1)} all-to-all(f32[8,2,128]{2,1,0:T(2,128)S(1)} %bitcast.11), channel_id=1, replica_groups=mesh['z'=16,'x'=4,'y'=4,'c'=2] {'y','c'}, dimensions={0} | all-to-all | bytes 16384 | tf_op jit(solution)/shard_map/all_to_all | solution.py:214
  123.5 0.6 reduce_sum.9
Async XLA Ops:
  6.5 103.6 %copy-start.2 = (s32[128]{0:T(128)S(1)}, s32[128]{0:T(128)}, u32[]{:S(2)}) copy-start(s32[128]{0:T(128)} %param.11) | copy-start | bytes 1540
  6.5 103.6 %copy-start.1 = (s32[128]{0:T(128)S(1)}, s32[128]{0:T(128)}, u32[]{:S(2)}) copy-start(s32[128]{0:T(128)} %param.10) | copy-start | bytes 1540
  6.5 103.6 %copy-start = (f32[1024]{0:T(1024)S(1)}, f32[1024]{0:T(1024)}, u32[]{:S(2)}) copy-start(f32[1024]{0:T(1024)} %param.8) | copy-start | bytes 12292
  6.5 103.6 %all-gather.2.cloned.1.call-start = ((), (), s32[]{:S(2)}) async-start(), calls=%async_computation.2 | async-start | bytes 4325376 | tf_op jit(solution)/shard_map/all_gather | solution.py:204
  6.5 27.4 %collective-permute-start.1 = (bf16[32,1024]{1,0:T(8,128)(2,1)}, bf16[32,1024]{1,0:T(8,128)(2,1)S(1)}, u32[]{:S(2)}, u32[]{:S(2)}) collective-permute-start(bf16[32,1024]{1,0:T(8,128)(2,1)} %bitcast.17), channel_id=1, source_target_pairs={{0,0},{33,1},{482,2},{67,3},{452,4},{101,5},{422,6},{135,7},{32,32... | collective-permute-start | bytes 196616 | tf_op jit(solution)/shard_map/ppermute | solution.py:200
  18.6 15.3 %collective-permute-start = (bf16[32,1024]{1,0:T(8,128)(2,1)}, bf16[32,1024]{1,0:T(8,128)(2,1)S(1)}, u32[]{:S(2)}, u32[]{:S(2)}) collective-permute-start(bf16[32,1024]{1,0:T(8,128)(2,1)} %bitcast.18), channel_id=1, source_target_pairs={{256,0},{289,1},{226,2},{323,3},{196,4},{357,5},{166,6},{391,7},{2... | collective-permute-start | bytes 196616 | tf_op jit(solution)/shard_map/ppermute | solution.py:200
  34.6 75.5 %all-to-all-start = ((bf16[512,8,128]{2,1,0:T(8,128)(2,1)}), bf16[512,8,128]{2,1,0:T(8,128)(2,1)S(1)}, u32[]{:S(2)}, u32[]{:S(2)}) async-start(bf16[512,8,128]{2,1,0:T(8,128)(2,1)} %bitcast.15), calls=%async_computation | async-start | bytes 2097152 | tf_op jit(solution)/shard_map/all_to_all | solution.py:205
Sparse Core Ops, SparseCore 0:
  34.7 62.0 all-gather.1

commit v9 on v8

--- a/solution.py
+++ b/solution.py
@@ -13,7 +13,7 @@
 EVERY = ("z", "x", "y", "c")
 MIB = 1 << 20
 NEAR = (0, 1, 15, 2, 14, 3, 13, 4)
-FAR = (8, 9, 7, 10, 6, 11, 5, 12)
+FAR = (8, 7, 9, 6, 10, 5, 11, 12)
 
 ERFC = (
     0.17087277,

time: 131 us -> 131 us (level)
    all_to_all x1, starting transfers between devices: 17.4 us -> 14.4 us  [body(): got = lax.all_to_all(sent.reshape(512, 8, 128), EVERY, 0, 0, tiled=True)]
    ppermute x2, starting transfers between devices: 15.8 us -> 18.6 us  [fetch(): return lax.ppermute(scen_weights.T, ('z', 'y', 'c'), ring)]
where the time goes in v9:
time: 131 us
  waiting for transfers between devices  58.1 us (44%)
  starting transfers between devices  33 us (25%)
  Pallas kernels  17.5 us (13%)
  between operations  13.5 us (10%)
  blocking collectives  7.43 us (6%)
  other arithmetic  1.32 us (1%)
    all_to_all x1, waiting for transfers between devices, body(): got = lax.all_to_all(sent.reshape(512, 8, 128), EVERY, 0, 0, tiled=True)  58 us
    ppermute x2, starting transfers between devices, fetch(): return lax.ppermute(scen_weights.T, ('z', 'y', 'c'), ring)  18.6 us
    all_to_all x1, starting transfers between devices, body(): got = lax.all_to_all(sent.reshape(512, 8, 128), EVERY, 0, 0, tiled=True)  14.4 us
    pallas_call x1, Pallas kernels, gather(): pl.pallas_call(gather_kernel, out_shape=jax.ShapeDtypeStruct((C // 2, 128...  11.6 us
    all_to_all x1, blocking collectives, body(): lax.all_to_all(part.reshape(8, 2, 128), ('y', 'c'), 0, 0, tiled=True)  7.43 us
    pallas_call x1, Pallas kernels, hazard_of(): pl.pallas_call(hazard_kernel, out_shape=jax.ShapeDtypeStruct((16, 128), j...  5.96 us
  transfers between devices with their start and end apart: 4, of which 1 were waited for; matrix products, arithmetic and copies ran while one was open for 0% of the time, Pallas kernels for 9%

profile of v9, /device:TPU:1, one launch (start us, length us, event | category | flops | bytes accessed | tf_op | source)
XLA Modules:
  0.0 130.8 jit_solution(13851468556973817944)
XLA Ops:
  6.5 0.0 copy-start.2
  6.5 0.0 copy-start.1
  6.5 0.0 copy-start
  6.5 0.0 all-gather.2.cloned.1.call-start
  6.5 12.1 %collective-permute-start.1 = (bf16[32,1024]{1,0:T(8,128)(2,1)}, bf16[32,1024]{1,0:T(8,128)(2,1)S(1)}, u32[]{:S(2)}, u32[]{:S(2)}) collective-permute-start(bf16[32,1024]{1,0:T(8,128)(2,1)} %bitcast.17), channel_id=1, source_target_pairs={{0,0},{33,1},{482,2},{67,3},{452,4},{101,5},{422,6},{135,7},{32,32... | collective-permute-start | bytes 196616 | tf_op jit(solution)/shard_map/ppermute | solution.py:200
  18.6 6.5 %collective-permute-start = (bf16[32,1024]{1,0:T(8,128)(2,1)}, bf16[32,1024]{1,0:T(8,128)(2,1)S(1)}, u32[]{:S(2)}, u32[]{:S(2)}) collective-permute-start(bf16[32,1024]{1,0:T(8,128)(2,1)} %bitcast.18), channel_id=1, source_target_pairs={{256,0},{225,1},{290,2},{195,3},{324,4},{165,5},{358,6},{391,7},{2... | collective-permute-start | bytes 196616 | tf_op jit(solution)/shard_map/ppermute | solution.py:200
  25.1 11.6 %gather_cells.1 = bf16[4096,128]{1,0:T(8,128)(2,1)} custom-call(s32[8192]{0:T(1024)} %cells_hbm.1, bf16[64,8192]{1,0:T(8,128)(2,1)} %bitcast.16), custom_call_target="tpu_custom_call" | custom-call | flops 1048576 | bytes 41943040 | tf_op jit(solution)/shard_map/gather_cells/pallas_call | solution.py:95
  36.7 0.0 collective-permute-done.1
  36.7 0.0 collective-permute-done
  36.8 0.7 pad_maximum_fusion
  37.4 0.0 all-gather.2.cloned.1.call-update
  37.4 14.4 %all-to-all-start = ((bf16[512,8,128]{2,1,0:T(8,128)(2,1)}), bf16[512,8,128]{2,1,0:T(8,128)(2,1)S(1)}, u32[]{:S(2)}, u32[]{:S(2)}) async-start(bf16[512,8,128]{2,1,0:T(8,128)(2,1)} %bitcast.15), calls=%async_computation | async-start | bytes 2097152 | tf_op jit(solution)/shard_map/all_to_all | solution.py:205
  51.8 0.1 pad_add_fusion.me_ref
  51.9 58.0 %all-to-all-done = bf16[512,8,128]{2,1,0:T(8,128)(2,1)S(1)} async-done(((bf16[512,8,128]{2,1,0:T(8,128)(2,1)}), bf16[512,8,128]{2,1,0:T(8,128)(2,1)S(1)}, u32[]{:S(2)}, u32[]{:S(2)}) %all-to-all-start) | async-done | bytes 1048608 | tf_op jit(solution)/shard_map/all_to_all | solution.py:205
  109.9 0.0 all-gather.2.cloned.1.call-done.weights_ref
  109.9 0.0 copy-done.2
  109.9 0.0 copy-done.1
  109.9 0.0 copy-done
  110.0 6.0 %hazard_levels.1 = f32[16,128]{1,0:T(8,128)S(1)} custom-call(s32[2]{0:T(128)S(1)} %pad_add_fusion.me_ref, bf16[4096,128]{1,0:T(8,128)(2,1)S(1)} %bitcast.10, bf16[2048,1024]{1,0:T(8,128)(2,1)} %all-gather.2.cloned.1.call-done.weights_ref, f32[1,1024]{1,0:T(1,128)S(1)} %bitcast.12, s32[1,128]{1,0:T(1,128)S(1)} %bitcast.13, s32[1,128]{1,0:T(1,128)S(1)} %bitcast.14), custom_call_target="tpu_custom_call" | custom-call | tf_op jit(solution)/shard_map/hazard_levels/pallas_call | solution.py:178
  115.9 7.4 %all_to_all.10 = f32[8,2,128]{2,1,0:T(2,128)S(1)} all-to-all(f32[8,2,128]{2,1,0:T(2,128)S(1)} %bitcast.11), channel_id=1, replica_groups=mesh['z'=16,'x'=4,'y'=4,'c'=2] {'y','c'}, dimensions={0} | all-to-all | bytes 16384 | tf_op jit(solution)/shard_map/all_to_all | solution.py:214
  123.4 0.6 reduce_sum.9
Async XLA Ops:
  6.5 103.4 %copy-start.2 = (s32[128]{0:T(128)S(1)}, s32[128]{0:T(128)}, u32[]{:S(2)}) copy-start(s32[128]{0:T(128)} %param.11) | copy-start | bytes 1540
  6.5 103.4 %copy-start.1 = (s32[128]{0:T(128)S(1)}, s32[128]{0:T(128)}, u32[]{:S(2)}) copy-start(s32[128]{0:T(128)} %param.10) | copy-start | bytes 1540
  6.5 103.4 %copy-start = (f32[1024]{0:T(1024)S(1)}, f32[1024]{0:T(1024)}, u32[]{:S(2)}) copy-start(f32[1024]{0:T(1024)} %param.8) | copy-start | bytes 12292
  6.5 103.4 %all-gather.2.cloned.1.call-start = ((), (), s32[]{:S(2)}) async-start(), calls=%async_computation.2 | async-start | bytes 4325376 | tf_op jit(solution)/shard_map/all_gather | solution.py:204
  6.5 30.2 %collective-permute-start.1 = (bf16[32,1024]{1,0:T(8,128)(2,1)}, bf16[32,1024]{1,0:T(8,128)(2,1)S(1)}, u32[]{:S(2)}, u32[]{:S(2)}) collective-permute-start(bf16[32,1024]{1,0:T(8,128)(2,1)} %bitcast.17), channel_id=1, source_target_pairs={{0,0},{33,1},{482,2},{67,3},{452,4},{101,5},{422,6},{135,7},{32,32... | collective-permute-start | bytes 196616 | tf_op jit(solution)/shard_map/ppermute | solution.py:200
  18.6 18.1 %collective-permute-start = (bf16[32,1024]{1,0:T(8,128)(2,1)}, bf16[32,1024]{1,0:T(8,128)(2,1)S(1)}, u32[]{:S(2)}, u32[]{:S(2)}) collective-permute-start(bf16[32,1024]{1,0:T(8,128)(2,1)} %bitcast.18), channel_id=1, source_target_pairs={{256,0},{225,1},{290,2},{195,3},{324,4},{165,5},{358,6},{391,7},{2... | collective-permute-start | bytes 196616 | tf_op jit(solution)/shard_map/ppermute | solution.py:200
  37.4 72.5 %all-to-all-start = ((bf16[512,8,128]{2,1,0:T(8,128)(2,1)}), bf16[512,8,128]{2,1,0:T(8,128)(2,1)S(1)}, u32[]{:S(2)}, u32[]{:S(2)}) async-start(bf16[512,8,128]{2,1,0:T(8,128)(2,1)} %bitcast.15), calls=%async_computation | async-start | bytes 2097152 | tf_op jit(solution)/shard_map/all_to_all | solution.py:205
Sparse Core Ops, SparseCore 0:
  37.6 59.0 all-gather.1

commit v10 on v9

--- a/solution.py
+++ b/solution.py
@@ -211,8 +211,7 @@
         level_base.reshape(1, 128),
         wet_mask.reshape(1, 128),
     )
-    hazard = lax.all_to_all(part.reshape(8, 2, 128), ("y", "c"), 0, 0, tiled=True)
-    return jnp.sum(hazard, axis=0)
+    return lax.psum_scatter(part, ("y", "c"), scatter_dimension=0, tiled=True)
 
 
 def solution(mesh):

time: 131 us -> 135 us (1.031)
  blocking collectives: 7.43 us -> 11.6 us
  waiting for transfers between devices: 58.1 us -> 55.9 us
  local copies, waits for them, and re-layouts: 0.01 us -> 1.92 us
    unnamed x0 -> x1, blocking collectives: none -> 11.6 us
    all_to_all x1 -> x0, blocking collectives: 7.43 us -> none  [body(): lax.all_to_all(part.reshape(8, 2, 128), ('y', 'c'), 0, 0, tiled=True)]
    all_to_all x1, waiting for transfers between devices: 58 us -> 55.9 us  [body(): got = lax.all_to_all(sent.reshape(512, 8, 128), EVERY, 0, 0, tiled=True)]
    unnamed x6 -> x8, local copies, waits for them, and re-layouts: 0.01 us -> 1.92 us
  transfers between devices with their start and end apart: 4 -> 4, of which waited for: 1 -> 1; matrix products, arithmetic and copies ran while one was open for 0% -> 1% of each run, Pallas kernels for 9% -> 9%
where the time goes in v10:
time: 135 us
  waiting for transfers between devices  55.9 us (41%)
  starting transfers between devices  32.9 us (24%)
  Pallas kernels  17.5 us (13%)
  between operations  14.2 us (11%)
  blocking collectives  11.6 us (9%)
  local copies, waits for them, and re-layouts  1.92 us (1%)
    all_to_all x1, waiting for transfers between devices, body(): got = lax.all_to_all(sent.reshape(512, 8, 128), EVERY, 0, 0, tiled=True)  55.9 us
    ppermute x2, starting transfers between devices, fetch(): return lax.ppermute(scen_weights.T, ('z', 'y', 'c'), ring)  18.6 us
    all_to_all x1, starting transfers between devices, body(): got = lax.all_to_all(sent.reshape(512, 8, 128), EVERY, 0, 0, tiled=True)  14.3 us
    unnamed x1, blocking collectives  11.6 us
    pallas_call x1, Pallas kernels, gather(): pl.pallas_call(gather_kernel, out_shape=jax.ShapeDtypeStruct((C // 2, 128...  11.6 us
    pallas_call x1, Pallas kernels, hazard_of(): pl.pallas_call(hazard_kernel, out_shape=jax.ShapeDtypeStruct((16, 128), j...  5.96 us
  transfers between devices with their start and end apart: 4, of which 1 were waited for; matrix products, arithmetic and copies ran while one was open for 1% of the time, Pallas kernels for 9%

profile of v10, /device:TPU:1, one launch (start us, length us, event | category | flops | bytes accessed | tf_op | source)
XLA Modules:
  0.0 134.8 jit_solution(6546326629221404556)
XLA Ops:
  6.5 0.0 copy-start
  6.5 0.0 copy-start.1
  6.5 0.0 copy-start.2
  6.5 0.0 all-gather.2.cloned.1.call-start
  6.5 16.0 %collective-permute-start = (bf16[32,1024]{1,0:T(8,128)(2,1)}, bf16[32,1024]{1,0:T(8,128)(2,1)S(1)}, u32[]{:S(2)}, u32[]{:S(2)}) collective-permute-start(bf16[32,1024]{1,0:T(8,128)(2,1)} %bitcast.16), channel_id=1, source_target_pairs={{256,0},{225,1},{290,2},{195,3},{324,4},{165,5},{358,6},{391,7},{2... | collective-permute-start | bytes 196616 | tf_op jit(solution)/shard_map/ppermute | solution.py:200
  22.5 2.6 %collective-permute-start.1 = (bf16[32,1024]{1,0:T(8,128)(2,1)}, bf16[32,1024]{1,0:T(8,128)(2,1)S(1)}, u32[]{:S(2)}, u32[]{:S(2)}) collective-permute-start(bf16[32,1024]{1,0:T(8,128)(2,1)} %bitcast.17), channel_id=1, source_target_pairs={{0,0},{33,1},{482,2},{67,3},{452,4},{101,5},{422,6},{135,7},{32,32... | collective-permute-start | bytes 196616 | tf_op jit(solution)/shard_map/ppermute | solution.py:200
  25.1 11.6 %gather_cells.1 = bf16[4096,128]{1,0:T(8,128)(2,1)} custom-call(s32[8192]{0:T(1024)} %cells_hbm.1, bf16[64,8192]{1,0:T(8,128)(2,1)} %bitcast.15), custom_call_target="tpu_custom_call" | custom-call | flops 1048576 | bytes 41943040 | tf_op jit(solution)/shard_map/gather_cells/pallas_call | solution.py:95
  36.7 0.0 collective-permute-done
  36.7 0.0 collective-permute-done.1
  36.8 0.7 pad_maximum_fusion
  37.4 0.0 all-gather.2.cloned.1.call-update
  37.4 14.3 %all-to-all-start = ((bf16[512,8,128]{2,1,0:T(8,128)(2,1)}), bf16[512,8,128]{2,1,0:T(8,128)(2,1)S(1)}, u32[]{:S(2)}, u32[]{:S(2)}) async-start(bf16[512,8,128]{2,1,0:T(8,128)(2,1)} %bitcast.14), calls=%async_computation | async-start | bytes 2097152 | tf_op jit(solution)/shard_map/all_to_all | solution.py:205
  51.8 1.3 dynamic-slice
  53.8 0.1 pad_add_fusion.me_ref
  53.9 55.9 %all-to-all-done = bf16[512,8,128]{2,1,0:T(8,128)(2,1)S(1)} async-done(((bf16[512,8,128]{2,1,0:T(8,128)(2,1)}), bf16[512,8,128]{2,1,0:T(8,128)(2,1)S(1)}, u32[]{:S(2)}, u32[]{:S(2)}) %all-to-all-start) | async-done | bytes 1048608 | tf_op jit(solution)/shard_map/all_to_all | solution.py:205
  109.8 0.0 all-gather.2.cloned.1.call-done.weights_ref
  109.8 0.0 copy-done
  109.8 0.0 copy-done.1
  109.8 0.0 copy-done.2
  109.8 6.0 %hazard_levels.1 = f32[16,128]{1,0:T(8,128)S(1)} custom-call(s32[2]{0:T(128)S(1)} %pad_add_fusion.me_ref, bf16[4096,128]{1,0:T(8,128)(2,1)S(1)} %bitcast.10, bf16[2048,1024]{1,0:T(8,128)(2,1)} %all-gather.2.cloned.1.call-done.weights_ref, f32[1,1024]{1,0:T(1,128)S(1)} %bitcast.11, s32[1,128]{1,0:T(1,128)S(1)} %bitcast.12, s32[1,128]{1,0:T(1,128)S(1)} %bitcast.13), custom_call_target="tpu_custom_call" | custom-call | tf_op jit(solution)/shard_map/hazard_levels/pallas_call | solution.py:178
  115.8 11.6 %all-reduce = f32[16,128]{1,0:T(8,128)S(1)} all-reduce(f32[16,128]{1,0:T(8,128)S(1)} %hazard_levels.1), channel_id=2, replica_groups=mesh['z'=16,'x'=4,'y'=4,'c'=2] {'y','c'}, use_global_device_ids=true, to_apply=%region_0.0.clone | all-reduce | flops 2048 | bytes 16384
  127.4 0.6 constant_dynamic-slice_fusion
Async XLA Ops:
  6.5 103.2 %copy-start = (f32[1024]{0:T(1024)S(1)}, f32[1024]{0:T(1024)}, u32[]{:S(2)}) copy-start(f32[1024]{0:T(1024)} %param.8) | copy-start | bytes 12292
  6.5 103.3 %copy-start.1 = (s32[128]{0:T(128)S(1)}, s32[128]{0:T(128)}, u32[]{:S(2)}) copy-start(s32[128]{0:T(128)} %param.10) | copy-start | bytes 1540
  6.5 103.3 %copy-start.2 = (s32[128]{0:T(128)S(1)}, s32[128]{0:T(128)}, u32[]{:S(2)}) copy-start(s32[128]{0:T(128)} %param.11) | copy-start | bytes 1540
  6.5 103.2 %all-gather.2.cloned.1.call-start = ((), (), s32[]{:S(2)}) async-start(), calls=%async_computation.1 | async-start | bytes 4325376 | tf_op jit(solution)/shard_map/all_gather | solution.py:204
  6.5 30.2 %collective-permute-start = (bf16[32,1024]{1,0:T(8,128)(2,1)}, bf16[32,1024]{1,0:T(8,128)(2,1)S(1)}, u32[]{:S(2)}, u32[]{:S(2)}) collective-permute-start(bf16[32,1024]{1,0:T(8,128)(2,1)} %bitcast.16), channel_id=1, source_target_pairs={{256,0},{225,1},{290,2},{195,3},{324,4},{165,5},{358,6},{391,7},{2... | collective-permute-start | bytes 196616 | tf_op jit(solution)/shard_map/ppermute | solution.py:200
  22.5 14.2 %collective-permute-start.1 = (bf16[32,1024]{1,0:T(8,128)(2,1)}, bf16[32,1024]{1,0:T(8,128)(2,1)S(1)}, u32[]{:S(2)}, u32[]{:S(2)}) collective-permute-start(bf16[32,1024]{1,0:T(8,128)(2,1)} %bitcast.17), channel_id=1, source_target_pairs={{0,0},{33,1},{482,2},{67,3},{452,4},{101,5},{422,6},{135,7},{32,32... | collective-permute-start | bytes 196616 | tf_op jit(solution)/shard_map/ppermute | solution.py:200
  37.4 72.3 %all-to-all-start = ((bf16[512,8,128]{2,1,0:T(8,128)(2,1)}), bf16[512,8,128]{2,1,0:T(8,128)(2,1)S(1)}, u32[]{:S(2)}, u32[]{:S(2)}) async-start(bf16[512,8,128]{2,1,0:T(8,128)(2,1)} %bitcast.14), calls=%async_computation | async-start | bytes 2097152 | tf_op jit(solution)/shard_map/all_to_all | solution.py:205
Sparse Core Ops, SparseCore 0:
  37.6 58.9 all-gather.1
